TPU v7x, 128 devices: a whole 4x4x4 slice. The times are simulated.
128 devices in a mesh: frames: 2 (over core), rows: 16 (over z, y), heads: 4 (over x).
Axes of the slice: x: 4, y: 4, z: 4, core: 2. Of those that a mesh axis runs over, the one named last changes fastest.
Arguments:
- queries: bfloat16 [2, 16, 2, 128, 5120], P('frames', 'rows', None, 'heads'), may hold values from -8 to 8
- keys: bfloat16 [2, 16, 2, 128, 5120], P('frames', 'rows', None, 'heads'), may hold values from -8 to 8
- values: bfloat16 [2, 16, 2, 128, 5120], P('frames', 'rows', None, 'heads'), may hold values from -6 to 6
- out_grad: bfloat16 [2, 16, 2, 128, 5120], P('frames', 'rows', None, 'heads'), may hold values from -6 to 6
- neighbours: int32 [2, 16, 2, 12], P('frames', 'rows'), may hold values from -1 to 63, as said below
Outputs:
- query_grad: bfloat16 [2, 16, 2, 128, 5120], P('frames', 'rows', None, 'heads')
- key_grad: bfloat16 [2, 16, 2, 128, 5120], P('frames', 'rows', None, 'heads')
- value_grad: bfloat16 [2, 16, 2, 128, 5120], P('frames', 'rows', None, 'heads')
Inputs may be any that keep to these rules, and one draw needn't show every extreme that they name: `neighbours`: each query tile lists, each once and in slots of no fixed order, the tiles of a box around it that reaches at most one tile along each of the three tile dimensions, always itself and always the tiles one row tile away, clipped at the grid's bounds; the other slots hold -1. Some query tile lists 12 tiles.
All inputs are finite; a program needn't handle non-finite values.
Results may differ from a plain program's by a relative error of at most 0.012.
Values may be sent and summed in bfloat16 or wider, within the bound.
A program may use at most 320 MiB of HBM per device.

v0:
```python
import jax
import jax.numpy as jnp
from jax import lax
from jax.sharding import PartitionSpec as P

HD = 128


def extended_2(x, sides, width):
    for axis, dim in sides:
        peers, length = (lax.axis_size(axis), x.shape[dim])
        up = [(i, (i + 1) % peers) for i in range(peers - 1)]
        down = [(j, i) for i, j in up]
        last = lax.slice_in_dim(x, length - width, length, axis=dim)
        first = lax.slice_in_dim(x, 0, width, axis=dim)
        before = lax.ppermute(last, axis, up)
        after = lax.ppermute(first, axis, down)
        x = jnp.concatenate([before, x, after], axis=dim)
    return x


def local(queries, keys, values, out_grad, neighbours):
    head_q, head_k, head_v, head_g = (
        lax.all_to_all(queries, "heads", split_axis=4, concat_axis=3, tiled=True),
        lax.all_to_all(keys, "heads", split_axis=4, concat_axis=3, tiled=True),
        lax.all_to_all(values, "heads", split_axis=4, concat_axis=3, tiled=True),
        lax.all_to_all(out_grad, "heads", split_axis=4, concat_axis=3, tiled=True),
    )
    frame_tiles, row_tiles, col_tiles, tile_tokens, channels = head_q.shape
    local_heads = channels // HD
    slot_count = neighbours.shape[-1]
    window_len = slot_count * tile_tokens
    query_count = frame_tiles * row_tiles * col_tiles
    ext_frames = frame_tiles + 2
    ext_rows = row_tiles + 2
    ext_count = ext_frames * ext_rows * col_tiles
    score_scale = HD ** (-0.5)
    split_shape = (frame_tiles, row_tiles, col_tiles, tile_tokens, local_heads, HD)
    query_major = head_q.reshape(split_shape).transpose(0, 1, 2, 4, 3, 5)
    grad_major = head_g.reshape(split_shape).transpose(0, 1, 2, 4, 3, 5)
    key_major = head_k.reshape(split_shape).transpose(4, 0, 1, 2, 3, 5)
    value_major = head_v.reshape(split_shape).transpose(4, 0, 1, 2, 3, 5)
    stacked = jnp.stack([key_major, value_major])
    extended = extended_2(stacked, (("frames", 2), ("rows", 3)), 1)
    ext_flat = extended.reshape(2, local_heads, ext_count, tile_tokens, HD)
    all_rows = row_tiles * lax.axis_size("rows")
    frame_start = lax.axis_index("frames") * frame_tiles
    row_start = lax.axis_index("rows") * row_tiles
    slot_table = neighbours.reshape(query_count, slot_count)
    global_frame = slot_table // (all_rows * col_tiles)
    global_row = slot_table // col_tiles % all_rows
    global_col = slot_table % col_tiles
    local_slot = (
        (global_frame - frame_start + 1) * ext_rows + global_row - row_start + 1
    ) * col_tiles + global_col
    local_slot = jnp.where(slot_table >= 0, local_slot, -1)
    query_rows = query_major.reshape(query_count, local_heads, tile_tokens, HD)
    grad_rows = grad_major.reshape(query_count, local_heads, tile_tokens, HD)

    def spread_mask(present):
        return jnp.broadcast_to(present[:, None], (slot_count, tile_tokens)).reshape(window_len)

    def tile_step(accumulated, inputs):
        query_tile, grad_tile, slots = inputs
        usable = slots >= 0
        safe_slots = jnp.where(usable, slots, 0)
        gathered = jnp.take(ext_flat, safe_slots, axis=2)
        gathered = gathered.reshape(2, local_heads, window_len, HD)
        window_keys = gathered[0]
        window_values = gathered[1]
        wide_mask = spread_mask(usable)[None, None, :]
        scores = (
            jnp.einsum("htd,hkd->htk", query_tile, window_keys, preferred_element_type=jnp.float32)
            * score_scale
        )
        scores = jnp.where(wide_mask, scores, -1e30)
        row_peak = jnp.max(scores, axis=-1, keepdims=True)
        weights = jnp.exp(scores - row_peak)
        total = jnp.sum(weights, axis=-1, keepdims=True)
        attention = weights / total
        attention_low = attention.astype(jnp.bfloat16)
        recomputed = jnp.einsum(
            "htk,hkd->htd", attention_low, window_values, preferred_element_type=jnp.float32
        )
        row_delta = jnp.sum(grad_tile.astype(jnp.float32) * recomputed, axis=-1)
        prob_grad = jnp.einsum(
            "htd,hkd->htk", grad_tile, window_values, preferred_element_type=jnp.float32
        )
        score_grad = (attention * (prob_grad - row_delta[:, :, None]) * score_scale).astype(
            jnp.bfloat16
        )
        query_grad = jnp.einsum(
            "htk,hkd->htd", score_grad, window_keys, preferred_element_type=jnp.float32
        ).astype(jnp.bfloat16)
        key_part = jnp.einsum(
            "htk,htd->hkd", score_grad, query_tile, preferred_element_type=jnp.float32
        )
        value_part = jnp.einsum(
            "htk,htd->hkd", attention_low, grad_tile, preferred_element_type=jnp.float32
        )
        slot_grads = jnp.stack([key_part, value_part]).reshape(
            2, local_heads, slot_count, tile_tokens * HD
        )
        slot_grads = jnp.where(usable[None, None, :, None], slot_grads, jnp.float32(0.0))
        accumulated = accumulated.at[:, :, safe_slots].add(slot_grads)
        row_stats = jnp.stack([row_peak[:, :, 0], total[:, :, 0], row_delta])
        return (accumulated, (query_grad, row_stats))

    initial = jnp.zeros((2, local_heads, ext_count, tile_tokens * HD), jnp.float32)
    accumulated, (query_grads, stat_rows) = lax.scan(
        tile_step, initial, (query_rows, grad_rows, local_slot)
    )
    grads = accumulated.reshape(2, local_heads, ext_frames, ext_rows, col_tiles, tile_tokens, HD)
    edge_slabs = jnp.concatenate([grads[:, :, :, :1], grads[:, :, :, -1:]], axis=3)
    received = extended_2(edge_slabs.astype(jnp.bfloat16), (("rows", 3),), 1).astype(
        edge_slabs.dtype
    )
    partial_value = grads[:, :, :, 1 : row_tiles + 1]
    partial_value = partial_value.at[:, :, :, 0].add(received[:, :, :, 0])
    partial_value = partial_value.at[:, :, :, -1].add(received[:, :, :, 3])
    edge_slabs = jnp.concatenate([partial_value[:, :, :1], partial_value[:, :, -1:]], axis=2)
    received = extended_2(edge_slabs.astype(jnp.bfloat16), (("frames", 2),), 1).astype(
        edge_slabs.dtype
    )
    folded = partial_value[:, :, 1 : frame_tiles + 1]
    folded = folded.at[:, :, 0].add(received[:, :, 0])
    folded = folded.at[:, :, -1].add(received[:, :, 3])
    token_shape = (frame_tiles, row_tiles, col_tiles, tile_tokens, channels)
    key_grad = folded[0].astype(jnp.bfloat16).transpose(1, 2, 3, 4, 0, 5).reshape(token_shape)
    value_grad = folded[1].astype(jnp.bfloat16).transpose(1, 2, 3, 4, 0, 5).reshape(token_shape)
    query_grad = (
        query_grads.reshape(frame_tiles, row_tiles, col_tiles, local_heads, tile_tokens, HD)
        .transpose(0, 1, 2, 4, 3, 5)
        .reshape(token_shape)
    )
    return (
        lax.all_to_all(query_grad, "heads", split_axis=3, concat_axis=4, tiled=True),
        lax.all_to_all(key_grad, "heads", split_axis=3, concat_axis=4, tiled=True),
        lax.all_to_all(value_grad, "heads", split_axis=3, concat_axis=4, tiled=True),
    )


def solution(mesh):
    in_specs = (
        P("frames", "rows", None, "heads", None),
        P("frames", "rows", None, "heads", None),
        P("frames", "rows", None, "heads", None),
        P("frames", "rows", None, "heads", None),
        P("frames", "rows", None, None),
    )
    out_specs = (
        P("frames", "rows", None, "heads", None),
        P("frames", "rows", None, "heads", None),
        P("frames", "rows", None, "heads", None),
    )
    return jax.shard_map(local, mesh=mesh, in_specs=in_specs, out_specs=out_specs, check_vma=False)
```

profile of v0, /device:TPU:24, one launch (start us, length us, event | category | flops | bytes accessed | tf_op | source)
XLA Modules:
  0.0 697.1 jit_solution(14547225356611103913)
XLA Ops:
  131.2 22.6 %collective-permute-done.3 = bf16[2,10,3,1,2,128,128]{6,5,4,3,2,1,0:T(8,128)(2,1)} collective-permute-done((bf16[2,10,3,1,2,128,128]{6,5,4,3,2,1,0:T(8,128)(2,1)}, bf16[2,10,3,1,2,128,128]{6,5,4,3,2,1,0:T(8,128)(2,1)}, u32[]{:S(2)}, u32[]{:S(2)}) %collective-permute-start.3) | collective-permute-done | bytes 3932192 | tf_op jit(solution)/shard_map/ppermute | solution.py:17
  176.4 10.7 %broadcast_in_dim.61 = f32[2,10,18,16384]{3,0,2,1:T(2,128)} broadcast(f32[]{:T(128)} %constant.177.clone.1), dimensions={} | broadcast | bytes 23592964 | tf_op jit(solution)/shard_map/broadcast_in_dim | solution.py:109
  187.2 315.8 %while.16 = (s32[]{:T(128)}, f32[2,10,18,16384]{3,0,2,1:T(2,128)}, bf16[2,10,128,128]{2,3,1,0:T(8,128)(2,1)S(1)}, s32[2,12]{1,0:T(2,128)S(1)}, bf16[2,10,128,128...) while((s32[]{:T(128)}, f32[2,10,18,16384]{3,0,2,1:T(2,128)}, ...), condition=%wide.region_5.6_spmd, body=%wide.region_0.5_spmd.sunk | while | flops 3057911296 | bytes 380804192 | solution.py:110
  187.5 9.2 %gather_fusion = bf16[12,2,10,128,128]{4,3,2,1,0:T(8,128)(2,1)} fusion(bf16[2,10,18,128,128]{4,3,2,1,0:T(8,128)(2,1)} %get-tuple-element.214, s32[1024]{0:T(1024)S(1)} %pad_clamp_fusion.2), kind=kCustom, calls=%fused_computation.clone.1 | custom fusion | bytes 15728688 | tf_op jit(solution)/shard_map/while/body/eval_jaxpr/jit(_take)/gather | solution.py:67
  205.7 7.8 %fusion.93 = (f32[10,128]{1,0:T(8,128)S(1)}, f32[10,128,1536]{2,1,0:T(8,128)}) fusion(pred[1536]{0:T(1024)(128)(4,1)S(1)} %broadcast_bitcast_fusion.2, bf16[10,1536,128]{2,1,0:T(8,128)(2,1)} %bitcast.192, bf16[2,10,128,128]{3,2,1,0:T(8,128)(2,1)S(1)} %get-tuple-element.213, s32[]{:T(128)S(6)} %copy.131), kind=kOutput, calls=%fused_computation.90.clone.1 | convolution fusion | flops 511182336 | bytes 12131332 | tf_op jit(solution)/shard_map/while/body/eval_jaxpr/sub | solution.py:78
  228.3 6.6 fusion.97
  234.9 9.0 %stack.24 = f32[1,10,12,16384]{3,2,1,0:T(8,128)} reshape(f32[10,1536,128]{2,1,0:T(8,128)} %fusion.97) | data formatting | bytes 15728640 | tf_op jit(solution)/shard_map/while/body/eval_jaxpr/stack | solution.py:101
  250.4 8.9 %stack.23 = f32[1,10,12,16384]{3,2,1,0:T(8,128)} reshape(f32[10,1536,128]{2,1,0:T(8,128)} %fusion.95) | data formatting | bytes 15728640 | tf_op jit(solution)/shard_map/while/body/eval_jaxpr/stack | solution.py:101
  259.4 15.9 %fusion.98 = f32[12,2,10,16384]{3,0,2,1:T(8,128)} fusion(f32[1,10,12,16384]{3,2,1,0:T(8,128)} %stack.23, f32[1,10,12,16384]{3,2,1,0:T(8,128)} %stack.24, pred[12]{0:T(512)(128)(4,1)S(1)} %get-tuple-element.187), kind=kLoop, calls=%fused_computation.4.clone.1 | loop fusion | flops 7864320 | bytes 31457292 | tf_op jit(solution)/shard_map/while/body/eval_jaxpr/jit(_where)/select_n | solution.py:104
  275.3 27.5 %copy.124 = f32[12,2,10,16384]{3,1,2,0:T(2,128)} copy(f32[12,2,10,16384]{3,0,2,1:T(8,128)} %fusion.98) | data formatting | bytes 31457280 | tf_op jit(solution)/shard_map/while/body/eval_jaxpr/jit(_where)/select_n | solution.py:104
  302.8 42.4 %scatter_fusion = f32[2,10,18,16384]{3,0,2,1:T(2,128)} fusion(f32[2,10,18,16384]{3,0,2,1:T(2,128)} %get-tuple-element.202, s32[12]{0:T(128)S(1)} %fusion.91, f32[12,2,10,16384]{3,1,2,0:T(2,128)} %copy.124), kind=kCustom, calls=%fused_computation.1.clone.1 | custom fusion | flops 3932160 | bytes 47185968 | tf_op jit(solution)/shard_map/while/body/eval_jaxpr/scatter-add | solution.py:105
  345.3 9.2 %gather_fusion = bf16[12,2,10,128,128]{4,3,2,1,0:T(8,128)(2,1)} fusion(bf16[2,10,18,128,128]{4,3,2,1,0:T(8,128)(2,1)} %get-tuple-element.214, s32[1024]{0:T(1024)S(1)} %pad_clamp_fusion.2), kind=kCustom, calls=%fused_computation.clone.1 | custom fusion | bytes 15728688 | tf_op jit(solution)/shard_map/while/body/eval_jaxpr/jit(_take)/gather | solution.py:67
  363.5 7.8 %fusion.93 = (f32[10,128]{1,0:T(8,128)S(1)}, f32[10,128,1536]{2,1,0:T(8,128)}) fusion(pred[1536]{0:T(1024)(128)(4,1)S(1)} %broadcast_bitcast_fusion.2, bf16[10,1536,128]{2,1,0:T(8,128)(2,1)} %bitcast.192, bf16[2,10,128,128]{3,2,1,0:T(8,128)(2,1)S(1)} %get-tuple-element.213, s32[]{:T(128)S(6)} %copy.131), kind=kOutput, calls=%fused_computation.90.clone.1 | convolution fusion | flops 511182336 | bytes 12131332 | tf_op jit(solution)/shard_map/while/body/eval_jaxpr/sub | solution.py:78
  386.1 6.6 fusion.97
  392.6 9.0 %stack.24 = f32[1,10,12,16384]{3,2,1,0:T(8,128)} reshape(f32[10,1536,128]{2,1,0:T(8,128)} %fusion.97) | data formatting | bytes 15728640 | tf_op jit(solution)/shard_map/while/body/eval_jaxpr/stack | solution.py:101
  408.2 8.9 %stack.23 = f32[1,10,12,16384]{3,2,1,0:T(8,128)} reshape(f32[10,1536,128]{2,1,0:T(8,128)} %fusion.95) | data formatting | bytes 15728640 | tf_op jit(solution)/shard_map/while/body/eval_jaxpr/stack | solution.py:101
  417.2 15.9 %fusion.98 = f32[12,2,10,16384]{3,0,2,1:T(8,128)} fusion(f32[1,10,12,16384]{3,2,1,0:T(8,128)} %stack.23, f32[1,10,12,16384]{3,2,1,0:T(8,128)} %stack.24, pred[12]{0:T(512)(128)(4,1)S(1)} %get-tuple-element.187), kind=kLoop, calls=%fused_computation.4.clone.1 | loop fusion | flops 7864320 | bytes 31457292 | tf_op jit(solution)/shard_map/while/body/eval_jaxpr/jit(_where)/select_n | solution.py:104
  433.1 27.5 %copy.124 = f32[12,2,10,16384]{3,1,2,0:T(2,128)} copy(f32[12,2,10,16384]{3,0,2,1:T(8,128)} %fusion.98) | data formatting | bytes 31457280 | tf_op jit(solution)/shard_map/while/body/eval_jaxpr/jit(_where)/select_n | solution.py:104
  460.6 42.1 %scatter_fusion = f32[2,10,18,16384]{3,0,2,1:T(2,128)} fusion(f32[2,10,18,16384]{3,0,2,1:T(2,128)} %get-tuple-element.202, s32[12]{0:T(128)S(1)} %fusion.91, f32[12,2,10,16384]{3,1,2,0:T(2,128)} %copy.124), kind=kCustom, calls=%fused_computation.1.clone.1 | custom fusion | flops 3932160 | bytes 47185968 | tf_op jit(solution)/shard_map/while/body/eval_jaxpr/scatter-add | solution.py:105
  503.0 30.7 %reshape.427 = f32[2,10,3,3,2,128,128]{6,5,0,4,3,2,1:T(8,128)} reshape(f32[2,10,18,16384]{3,0,2,1:T(2,128)} %get-tuple-element.90) | data formatting | bytes 47185920 | tf_op jit(solution)/shard_map/reshape | solution.py:113
  533.6 9.1 %convert.18 = bf16[2,10,3,3,2,128,128]{6,5,0,4,3,2,1:T(8,128)(2,1)S(1)} convert(f32[2,10,3,3,2,128,128]{6,5,0,4,3,2,1:T(8,128)} %reshape.427) | non-fusion elementwise | flops 5898240 | bytes 35389440 | tf_op jit(solution)/shard_map/convert.10
  549.6 82.7 %collective-permute-done.4 = bf16[2,10,3,1,2,128,128]{6,5,0,4,3,2,1:T(8,128)(2,1)S(1)} collective-permute-done((bf16[2,10,3,1,2,128,128]{6,5,0,4,3,2,1:T(8,128)(2,1)S(1)}, bf16[2,10,3,1,2,128,128]{6,5,0,4,3,2,1:T(8,128)(2,1)S(1)}, u32[]{:S(2)}, u32[]{:S(2)}) %collective-permute-start.4) | collective-permute-done | bytes 3932192 | tf_op jit(solution)/shard_map/ppermute | solution.py:16
  670.9 9.9 %all-to-all-done.6 = bf16[1,1,2,128,1280]{4,2,1,0,3:T(2,128)(2,1)S(1)} async-done(((bf16[1,1,2,128,1280]{4,2,1,0,3:T(2,128)(2,1)}), bf16[1,1,2,128,1280]{4,2,1,0,3:T(2,128)(2,1)S(1)}, u32[]{:S(2)}, u32[]{:S(2)}) %all-to-all-start.6) | async-done | bytes 655392 | tf_op jit(solution)/shard_map/all_to_all | solution.py:139
  686.2 9.5 %all-to-all-done.5 = bf16[1,1,2,128,1280]{4,2,1,0,3:T(2,128)(2,1)S(1)} async-done(((bf16[1,1,2,128,1280]{4,2,1,0,3:T(2,128)(2,1)}), bf16[1,1,2,128,1280]{4,2,1,0,3:T(2,128)(2,1)S(1)}, u32[]{:S(2)}, u32[]{:S(2)}) %all-to-all-start.5) | async-done | bytes 655392 | tf_op jit(solution)/shard_map/all_to_all | solution.py:138
  (147 shorter events, 265.2 us)
Async XLA Ops:
  8.6 15.2 %all-to-all-start.1 = ((bf16[4,2,40960]{2,1,0:T(2,128)(2,1)}), bf16[4,2,40960]{2,1,0:T(2,128)(2,1)S(1)}, u32[]{:S(2)}, u32[]{:S(2)}) async-start(bf16[4,2,40960]{2,1,0:T(2,128)(2,1)} %reshape.450), calls=%async_computation.1 | async-start | bytes 1310720 | tf_op jit(solution)/shard_map/all_to_all | solution.py:25
  23.8 14.2 %all-to-all-start.2 = ((bf16[4,2,40960]{2,1,0:T(2,128)(2,1)}), bf16[4,2,40960]{2,1,0:T(2,128)(2,1)}, u32[]{:S(2)}, u32[]{:S(2)}) async-start(bf16[4,2,40960]{2,1,0:T(2,128)(2,1)} %reshape.448), calls=%async_computation.2 | async-start | bytes 1310720 | tf_op jit(solution)/shard_map/all_to_all | solution.py:26
  47.7 5.3 copy-start.8
  48.4 4.9 collective-permute-start.1
  49.7 5.8 collective-permute-start
  62.3 91.5 %collective-permute-start.3 = (bf16[2,10,3,1,2,128,128]{6,5,4,3,2,1,0:T(8,128)(2,1)}, bf16[2,10,3,1,2,128,128]{6,5,4,3,2,1,0:T(8,128)(2,1)}, u32[]{:S(2)}, u32[]{:S(2)}) collective-permute-start(bf16[2,10,3,1,2,128,128]{6,5,4,3,2,1,0:T(8,128)(2,1)} %copy.83), channel_id=1, source_target_pairs={{4,0},{8,4},{12,8},{16,12},{20,16},{24,20},{28,24},{32,28},{36,32}... | collective-permute-start | bytes 11796488 | tf_op jit(solution)/shard_map/ppermute | solution.py:17
  65.0 94.3 %collective-permute-start.2 = (bf16[2,10,3,1,2,128,128]{6,5,4,3,2,1,0:T(8,128)(2,1)}, bf16[2,10,3,1,2,128,128]{6,5,4,3,2,1,0:T(8,128)(2,1)}, u32[]{:S(2)}, u32[]{:S(2)}) collective-permute-start(bf16[2,10,3,1,2,128,128]{6,5,4,3,2,1,0:T(8,128)(2,1)} %copy.83), channel_id=1, source_target_pairs={{0,4},{4,8},{8,12},{12,16},{16,20},{20,24},{24,28},{28,32},{32,36}... | collective-permute-start | bytes 11796488 | tf_op jit(solution)/shard_map/ppermute | solution.py:16
  81.3 15.3 %all-to-all-start = ((bf16[4,2,40960]{2,1,0:T(2,128)(2,1)}), bf16[4,2,40960]{2,1,0:T(2,128)(2,1)}, u32[]{:S(2)}, u32[]{:S(2)}) async-start(bf16[4,2,40960]{2,1,0:T(2,128)(2,1)} %reshape.446), calls=%async_computation | async-start | bytes 1310720 | tf_op jit(solution)/shard_map/all_to_all | solution.py:24
  85.5 16.0 %copy-start.14 = (s32[1,1,2,12]{3,2,1,0:T(2,128)S(1)}, s32[1,1,2,12]{3,2,1,0:T(2,128)}, u32[]{:S(2)}) copy-start(s32[1,1,2,12]{3,2,1,0:T(2,128)} %param.19) | copy-start | bytes 292
  96.6 19.7 %all-to-all-start.3 = ((bf16[4,2,40960]{2,1,0:T(2,128)(2,1)}), bf16[4,2,40960]{2,1,0:T(2,128)(2,1)}, u32[]{:S(2)}, u32[]{:S(2)}) async-start(bf16[4,2,40960]{2,1,0:T(2,128)(2,1)} %reshape.452), calls=%async_computation.3 | async-start | bytes 1310720 | tf_op jit(solution)/shard_map/all_to_all | solution.py:27
  159.2 5.6 copy-start.7
  159.2 5.6 copy-start.10
  176.4 10.7 %copy-start.11 = (bf16[2,10,128,128]{3,2,1,0:T(8,128)(2,1)S(1)}, bf16[2,10,128,128]{3,2,1,0:T(8,128)(2,1)}, u32[]{:S(2)}) copy-start(bf16[2,10,128,128]{3,2,1,0:T(8,128)(2,1)} %copy.89) | copy-start | bytes 1966084
  176.4 10.7 %copy-start.12 = (bf16[2,10,128,128]{3,2,1,0:T(8,128)(2,1)S(1)}, bf16[2,10,128,128]{3,2,1,0:T(8,128)(2,1)}, u32[]{:S(2)}) copy-start(bf16[2,10,128,128]{3,2,1,0:T(8,128)(2,1)} %copy.91) | copy-start | bytes 1966084
  176.4 10.7 %copy-start.13 = (bf16[2,10,128,128]{2,3,1,0:T(8,128)(2,1)S(1)}, bf16[2,10,128,128]{2,3,1,0:T(8,128)(2,1)}, u32[]{:S(2)}) copy-start(bf16[2,10,128,128]{2,3,1,0:T(8,128)(2,1)} %custom-call.2) | copy-start | bytes 1966084
  213.6 6.4 copy-start.4
  371.4 6.4 copy-start.4
  543.8 88.5 %collective-permute-start.4 = (bf16[2,10,3,1,2,128,128]{6,5,0,4,3,2,1:T(8,128)(2,1)S(1)}, bf16[2,10,3,1,2,128,128]{6,5,0,4,3,2,1:T(8,128)(2,1)S(1)}, u32[]{:S(2)}, u32[]{:S(2)}) collective-permute-start(bf16[2,10,3,1,2,128,128]{6,5,0,4,3,2,1:T(8,128)(2,1)S(1)} %get-tuple-element.132), channel_id=1, source_target_pairs={{0,4},{4,8},{8,12},{12,16},{16,20},{20,24},{24,28},{28,32},{32,36}... | collective-permute-start | bytes 11796488 | tf_op jit(solution)/shard_map/ppermute | solution.py:16
  546.2 90.1 %collective-permute-start.5 = (bf16[2,10,3,1,2,128,128]{6,5,0,4,3,2,1:T(8,128)(2,1)S(1)}, bf16[2,10,3,1,2,128,128]{6,5,0,4,3,2,1:T(8,128)(2,1)S(1)}, u32[]{:S(2)}, u32[]{:S(2)}) collective-permute-start(bf16[2,10,3,1,2,128,128]{6,5,0,4,3,2,1:T(8,128)(2,1)S(1)} %get-tuple-element.133), channel_id=1, source_target_pairs={{4,0},{8,4},{12,8},{16,12},{20,16},{24,20},{28,24},{32,28},{36,32}... | collective-permute-start | bytes 11796488 | tf_op jit(solution)/shard_map/ppermute | solution.py:17
  645.2 9.3 %collective-permute-start.6 = (bf16[2,10,1,1,2,128,128]{6,5,0,4,1,2,3:T(8,128)(2,1)S(1)}, bf16[2,10,1,1,2,128,128]{6,5,0,4,1,2,3:T(8,128)(2,1)}, u32[]{:S(2)}, u32[]{:S(2)}) collective-permute-start(bf16[2,10,1,1,2,128,128]{6,5,0,4,1,2,3:T(8,128)(2,1)S(1)} %get-tuple-element.134), channel_id=1, source_target_pairs={{0,64},{1,65},{2,66},{3,67},{4,68},{5,69},{6,70},{7,71},{8,72},{9,... | collective-permute-start | bytes 3932168 | tf_op jit(solution)/shard_map/ppermute | solution.py:16
  647.6 6.9 collective-permute-start.7
  650.8 14.4 %all-to-all-start.4 = ((bf16[1,1,2,128,1280]{4,2,1,0,3:T(2,128)(2,1)}), bf16[1,1,2,128,1280]{4,2,1,0,3:T(2,128)(2,1)S(1)}, u32[]{:S(2)}, u32[]{:S(2)}) async-start(bf16[1,1,2,128,1280]{4,2,1,0,3:T(2,128)(2,1)} %copy.93), calls=%async_computation.4 | async-start | bytes 1310720 | tf_op jit(solution)/shard_map/all_to_all | solution.py:137
  665.2 15.6 %all-to-all-start.6 = ((bf16[1,1,2,128,1280]{4,2,1,0,3:T(2,128)(2,1)}), bf16[1,1,2,128,1280]{4,2,1,0,3:T(2,128)(2,1)S(1)}, u32[]{:S(2)}, u32[]{:S(2)}) async-start(bf16[1,1,2,128,1280]{4,2,1,0,3:T(2,128)(2,1)} %copy.104), calls=%async_computation.6 | async-start | bytes 1310720 | tf_op jit(solution)/shard_map/all_to_all | solution.py:139
  680.8 14.9 %all-to-all-start.5 = ((bf16[1,1,2,128,1280]{4,2,1,0,3:T(2,128)(2,1)}), bf16[1,1,2,128,1280]{4,2,1,0,3:T(2,128)(2,1)S(1)}, u32[]{:S(2)}, u32[]{:S(2)}) async-start(bf16[1,1,2,128,1280]{4,2,1,0,3:T(2,128)(2,1)} %copy.100), calls=%async_computation.5 | async-start | bytes 1310720 | tf_op jit(solution)/shard_map/all_to_all | solution.py:138
  (11 other events, 30.1 us)
where the time goes:
time: 709 us; the launch traced here: 697 us
  local copies, waits for them, and re-layouts  294 us (41%)
  other arithmetic  158 us (22%)
  waiting for transfers between devices  143 us (20%)
  matrix products  50.3 us (7%)
  starting transfers between devices  49.8 us (7%)
    scatter-add x2, other arithmetic, tile_step(): accumulated = accumulated.at[:, :, safe_slots].add(slot_grads)  84.5 us
    ppermute x4, waiting for transfers between devices, extended_2(): before = lax.ppermute(last, axis, up)  83.8 us
    unnamed x32, local copies, waits for them, and re-layouts  56.8 us
    select_n x2, local copies, waits for them, and re-layouts, tile_step(): jnp.where(usable[None, None, :, None], slot_grads, jnp.float32(0.0))  55.1 us
    another operation x4, local copies, waits for them, and re-layouts, tile_step(): jnp.stack([key_part, value_part])  35.9 us
    select_n x2, other arithmetic, tile_step(): jnp.where(usable[None, None, :, None], slot_grads, jnp.float32(0.0))  31.8 us
    reshape x1, local copies, waits for them, and re-layouts, local(): accumulated.reshape(2, local_heads, ext_frames, ext_rows, col_tiles, tile...  30.7 us
    ppermute x4, waiting for transfers between devices, extended_2(): after = lax.ppermute(first, axis, down)  27.1 us
  transfers between devices with their start and end apart: 15, of which 11 were waited for; matrix products, arithmetic and copies ran while one was open for 12% of the time, Pallas kernels for 0%

commit v1 on v0

v1 whole, which is shorter than its diff:
```python
import functools

import jax
import jax.numpy as jnp
from jax import lax
from jax.experimental import pallas as pl
from jax.experimental.pallas import tpu as pltpu
from jax.sharding import PartitionSpec as P

MESH = pl.DeviceIdType.MESH
HD = 128
TILE = 128
NROWS = 16
LOG2E = 1.4426950408889634
NONE = -1e30
NT = (((1,), (1,)), ((), ()))
NN = (((1,), (0,)), ((), ()))
TN = (((0,), (0,)), ((), ()))


def dot(a, b, dims):
    return lax.dot_general(a, b, dims, preferred_element_type=jnp.float32)


def phase_a(j, p, qg, kv, bias, es, dps, ms, pst):
    scale = LOG2E * HD**-0.5

    def block(i, carry):
        s, f = i // 2, i % 2
        q = qg[s, j, 0, f].reshape(2 * TILE, HD)
        g = qg[s, j, 1, f].reshape(2 * TILE, HD)
        peaks, sums, prods = [], [], []
        for kt in range(4):
            k = kv[j, 0, kt // 2, kt % 2].reshape(TILE, HD)
            v = kv[j, 1, kt // 2, kt % 2].reshape(TILE, HD)
            st = dot(k, q, NT) * scale
            m = jnp.max(st, axis=0, keepdims=True)
            e = jnp.exp2(st - m)
            dp = dot(v, g, NT)
            es[p, i, kt] = e
            dps[p, i, kt] = dp
            mb = m + bias[s, f, kt : kt + 1, :]
            ms[p, i, kt : kt + 1, :] = mb
            peaks.append(mb)
            sums.append(jnp.sum(e, axis=0, keepdims=True))
            prods.append(jnp.sum(e * dp, axis=0, keepdims=True))
        top = functools.reduce(jnp.maximum, peaks)
        ws = [jnp.exp2(mb - top) for mb in peaks]
        pst[j, s, f, 0:1, :] = top
        pst[j, s, f, 1:2, :] = sum(w * l for w, l in zip(ws, sums))
        pst[j, s, f, 2:3, :] = sum(w * d for w, d in zip(ws, prods))
        return carry

    lax.fori_loop(0, 6, block, 0)


def combine(j, pst, prc, fin):
    for f in range(2):
        parts = [pst[j, 1, f], prc[j, 0, f], prc[j, 1, f]]
        top = functools.reduce(jnp.maximum, [x[0:1] for x in parts])
        ws = [jnp.exp2(x[0:1] - top) for x in parts]
        total = sum(w * x[1:2] for w, x in zip(ws, parts))
        prod = sum(w * x[2:3] for w, x in zip(ws, parts))
        fin[j, 1, f, 0:1, :] = top + jnp.log2(total)
        fin[j, 1, f, 1:2, :] = prod / total


def phase_b(j, p, qg, kv, es, dps, ms, fin, dka, dva, dqs, dqf, ost):
    scale = HD**-0.5
    dka[...] = jnp.zeros_like(dka)
    dva[...] = jnp.zeros_like(dva)

    def block(i, carry):
        s, f = i // 2, i % 2
        q = qg[s, j, 0, f].reshape(2 * TILE, HD)
        g = qg[s, j, 1, f].reshape(2 * TILE, HD)
        lse = fin[j, s, f, 0:1, :]
        delta = fin[j, s, f, 1:2, :]
        dq = jnp.zeros((2 * TILE, HD), jnp.float32)
        for kt in range(4):
            k = kv[j, 0, kt // 2, kt % 2].reshape(TILE, HD)
            r = jnp.exp2(ms[p, i, kt : kt + 1, :] - lse)
            prob = es[p, i, kt] * r
            ds = (prob * (dps[p, i, kt] - delta)).astype(jnp.bfloat16)
            dva[kt] += dot(prob.astype(jnp.bfloat16), g, NN)
            dka[kt] += dot(ds, q, NN)
            dq += dot(ds, k, TN)
        dq = dq * scale
        rows = pl.ds(pl.multiple_of(f * 2 * TILE, 2 * TILE), 2 * TILE)
        dqs[j, s, rows] = dq.astype(jnp.bfloat16)

        @pl.when(s == 1)
        def _():
            dqf[j, rows] = dq

        return carry

    lax.fori_loop(0, 6, block, 0)
    ost[j, 1] = (dka[...] * scale).astype(jnp.bfloat16).reshape(ost.shape[2:])
    ost[j, 2] = dva[...].astype(jnp.bfloat16).reshape(ost.shape[2:])


def kernel(nh, q_ref, k_ref, v_ref, g_ref, nb_ref, oq_ref, ok_ref, ov_ref,
           qg, kv, tab, bias, es, dps, ms, pst, prc, fin, dka, dva, dqs, dqr, dqf, ost,
           xin_s, xin_r, halo_s, halo_r, part_s, part_r, fin_s, fin_r, dq_s, dq_r, out_s, out_r,
           tab_s, tab_r, bias_s, bias_r):
    f = lax.axis_index("frames")
    h = lax.axis_index("rows")
    x = lax.axis_index("heads")
    me = x * 2 + f
    up, down = lax.rem(h + NROWS - 1, NROWS), lax.rem(h + 1, NROWS)
    beside = (f, up, x), (f, down, x)

    def member(k):
        other = lax.rem(me + k, 8)
        return other, (other % 2, h, other // 2)

    barrier = pltpu.get_barrier_semaphore()
    for device in [member(k)[1] for k in range(1, 8)] + list(beside):
        pl.semaphore_signal(barrier, inc=1, device_id=device, device_id_type=MESH)
    pl.semaphore_wait(barrier, 9)

    def remote(src, dst, send, recv, device):
        return pltpu.make_async_remote_copy(
            src_ref=src, dst_ref=dst, send_sem=send, recv_sem=recv, device_id=device, device_id_type=MESH
        )

    def await_bytes(ref, sem):
        pltpu.make_async_copy(ref, ref, sem).wait()

    def lanes(owner, j):
        return pl.ds(pl.multiple_of((owner * nh + j) * HD, HD), HD)

    def enter(j):
        for a, (src, dst) in enumerate(((q_ref, qg.at[1, j, 0]), (g_ref, qg.at[1, j, 1]),
                                        (k_ref, kv.at[j, 0]), (v_ref, kv.at[j, 1]))):
            to = dst.at[f, :, x]
            recv = xin_r.at[j, a // 2]
            pltpu.make_async_copy(src.at[0, 0, :, :, lanes(me, j)], to, recv).start()
            for k in range(1, 8):
                other, device = member(k)
                remote(src.at[0, 0, :, :, lanes(other, j)], to, xin_s.at[j, a], recv, device).start()

    def leave(j, a, out):
        to = out.at[0, 0, :, :, lanes(me, j)]
        pltpu.make_async_copy(ost.at[j, a, f, :, x], to, out_r.at[a]).start()
        for k in range(1, 8):
            other, device = member(k)
            remote(ost.at[j, a, other % 2, :, other // 2], to, out_s.at[j, a], out_r.at[a], device).start()

    lax.fori_loop(0, nh, lambda j, c: (enter(j), c)[1], 0)

    for n, dr in enumerate((1, 0, -1)):
        row = h + dr
        inside = jnp.logical_and(row >= 0, row < NROWS)
        for kt in range(4):
            wanted = jnp.where(inside, (kt // 2 * NROWS + row) * 2 + kt % 2, -2)
            for c in range(2):
                found = jnp.where(nb_ref[0, 0, c : c + 1, :] == wanted, 0.0, NONE)
                found = jnp.max(found, axis=-1, keepdims=True)
                tab[n, f, kt : kt + 1, c * TILE : (c + 1) * TILE] = jnp.broadcast_to(found, (1, TILE))
        tab[n, f, 4:8, :] = jnp.zeros((4, 2 * TILE), jnp.float32)
    swap = remote(tab.at[:, f], tab.at[:, f], tab_s, tab_r, (1 - f, h, x))
    swap.start()
    swap.wait()
    bias[1] = tab[1]
    lend = [remote(tab.at[2 * n], bias.at[2 * n], bias_s.at[n], bias_r.at[n], beside[1 - n]) for n in range(2)]
    for copy in lend:
        copy.start()

    def step(t, carry):
        @pl.when(t < nh)
        def _():
            j = t
            await_bytes(qg.at[1, j], xin_r.at[j, 0])
            for n in range(2):
                remote(qg.at[1, j], qg.at[2 * n, j], halo_s.at[n, j], halo_r.at[n, j], beside[1 - n]).start()

        @pl.when(jnp.logical_and(t >= 2, t < nh + 2))
        def _():
            j = t - 2
            for n in range(2):
                await_bytes(prc.at[j, n], part_r.at[n, j])
            combine(j, pst, prc, fin)
            for n in range(2):
                remote(fin.at[j, 1], fin.at[j, 2 * n], fin_s.at[n, j], fin_r.at[n, j], beside[1 - n]).start()

        @pl.when(jnp.logical_and(t >= 1, t < nh + 1))
        def _():
            j = t - 1

            @pl.when(t == 1)
            def _():
                for copy in lend:
                    copy.wait_recv()

            await_bytes(kv.at[j], xin_r.at[j, 1])
            for n in range(2):
                await_bytes(qg.at[2 * n, j], halo_r.at[n, j])
            phase_a(j, j % 2, qg, kv, bias, es, dps, ms, pst)
            for n in range(2):
                remote(pst.at[j, 2 * n], prc.at[j, 1 - n], part_s.at[n, j], part_r.at[1 - n, j], beside[n]).start()

        @pl.when(jnp.logical_and(t >= 2, t < nh + 2))
        def _():
            j = t - 2
            for n in range(2):
                await_bytes(fin.at[j, 2 * n], fin_r.at[n, j])
            phase_b(j, j % 2, qg, kv, es, dps, ms, fin, dka, dva, dqs, dqf, ost)
            for n in range(2):
                remote(dqs.at[j, 2 * n], dqr.at[j, 1 - n], dq_s.at[n, j], dq_r.at[1 - n, j], beside[n]).start()
            leave(j, 1, ok_ref)
            leave(j, 2, ov_ref)

        @pl.when(t >= 3)
        def _():
            j = t - 3
            for n in range(2):
                await_bytes(dqr.at[j, n], dq_r.at[n, j])
            total = dqf[j] + dqr[j, 0].astype(jnp.float32) + dqr[j, 1].astype(jnp.float32)
            ost[j, 0] = total.astype(jnp.bfloat16).reshape(ost.shape[2:])
            leave(j, 0, oq_ref)

        return carry

    lax.fori_loop(0, nh + 3, step, 0)

    for a, out in enumerate((oq_ref, ok_ref, ov_ref)):
        await_bytes(out, out_r.at[a])
    for copy in lend:
        copy.wait_send()

    def settle(j, carry):
        sent = dqs.at[j, 0, pl.ds(0, 7 * TILE // 2)]
        for a in range(4):
            await_bytes(sent, xin_s.at[j, a])
        for a in range(3):
            await_bytes(sent, out_s.at[j, a])
        for n in range(2):
            await_bytes(qg.at[1, j], halo_s.at[n, j])
            await_bytes(prc.at[j, n], part_s.at[n, j])
            await_bytes(prc.at[j, n], fin_s.at[n, j])
            await_bytes(dqr.at[j, n], dq_s.at[n, j])
        return carry

    lax.fori_loop(0, nh, settle, 0)


def local(queries, keys, values, out_grad, neighbours):
    nh = queries.shape[-1] // HD // 8
    tiles = (2, 2, 4, TILE // 4, HD)
    bf, f32 = jnp.bfloat16, jnp.float32
    dma = pltpu.SemaphoreType.DMA
    any_spec = pl.BlockSpec(memory_space=pl.ANY)
    shape = jax.ShapeDtypeStruct(queries.shape, bf)
    products = 5 * 512 * 1536 * HD * nh
    return pl.pallas_call(
        functools.partial(kernel, nh),
        out_shape=(shape, shape, shape),
        in_specs=[any_spec] * 4 + [pl.BlockSpec(memory_space=pltpu.VMEM)],
        out_specs=[any_spec] * 3,
        scratch_shapes=[
            pltpu.VMEM((3, nh, 2) + tiles, bf),
            pltpu.VMEM((nh, 2) + tiles, bf),
            pltpu.VMEM((3, 2, 8, 256), f32),
            pltpu.VMEM((3, 2, 8, 256), f32),
            pltpu.VMEM((2, 6, 4, TILE, 256), f32),
            pltpu.VMEM((2, 6, 4, TILE, 256), f32),
            pltpu.VMEM((2, 6, 8, 256), f32),
            pltpu.VMEM((nh, 3, 2, 8, 256), f32),
            pltpu.VMEM((nh, 2, 2, 8, 256), f32),
            pltpu.VMEM((nh, 3, 2, 8, 256), f32),
            pltpu.VMEM((4, TILE, HD), f32),
            pltpu.VMEM((4, TILE, HD), f32),
            pltpu.VMEM((nh, 3, 512, HD), bf),
            pltpu.VMEM((nh, 2, 512, HD), bf),
            pltpu.VMEM((nh, 512, HD), f32),
            pltpu.VMEM((nh, 3) + tiles, bf),
            dma((nh, 4)), dma((nh, 2)),
            dma((2, nh)), dma((2, nh)),
            dma((2, nh)), dma((2, nh)),
            dma((2, nh)), dma((2, nh)),
            dma((2, nh)), dma((2, nh)),
            dma((nh, 3)), dma((3,)),
            dma(()), dma(()),
            dma((2,)), dma((2,)),
        ],
        compiler_params=pltpu.CompilerParams(
            collective_id=0, has_side_effects=True, vmem_limit_bytes=48 * 1024 * 1024
        ),
        cost_estimate=pl.CostEstimate(
            flops=2 * products, bytes_accessed=7 * 2 * queries.size, transcendentals=512 * 1536 * nh
        ),
        name="window_backward",
    )(queries, keys, values, out_grad, neighbours)


def solution(mesh):
    whole = P("frames", "rows", None, "heads", None)
    return jax.shard_map(
        local,
        mesh=mesh,
        in_specs=(whole, whole, whole, whole, P("frames", "rows", None, None)),
        out_specs=(whole, whole, whole),
        check_vma=False,
    )
```

time: 709 us -> 102 us (0.14)
  the two profiles are of different devices: /device:TPU:24 before, /device:TPU:1 now
where the time goes in v1:
time: 102 us
  Pallas kernels  93.7 us (92%)
  local copies, waits for them, and re-layouts  7.53 us (7%)
    pallas_call x1, Pallas kernels, local(): pl.pallas_call(functools.partial(kernel, nh), out_shape=(shape, shape, sh...  93.7 us
    unnamed x13, local copies, waits for them, and re-layouts  7.53 us

profile of v1, /device:TPU:1, one launch (start us, length us, event | category | flops | bytes accessed | tf_op | source)
XLA Modules:
  0.0 101.9 jit_solution(1509922561121294113)
XLA Ops:
  0.6 0.0 copy-start
  0.6 1.1 %copy-done = bf16[1,1,2,32,5120]{4,3,2,1,0:T(8,128)(2,1)S(1)} copy-done((bf16[1,1,2,32,5120]{4,3,2,1,0:T(8,128)(2,1)S(1)}, bf16[1,1,2,32,5120]{4,3,2,1,0:T(8,128)(2,1)}, u32[]{:S(2)}) %copy-start) | copy-done | bytes 655384
  1.7 0.0 copy-start.1
  1.7 1.1 %copy-done.1 = bf16[1,1,2,32,5120]{4,3,2,1,0:T(8,128)(2,1)S(1)} copy-done((bf16[1,1,2,32,5120]{4,3,2,1,0:T(8,128)(2,1)S(1)}, bf16[1,1,2,32,5120]{4,3,2,1,0:T(8,128)(2,1)}, u32[]{:S(2)}) %copy-start.1) | copy-done | bytes 655384
  2.8 0.0 copy-start.2
  2.8 1.1 %copy-done.2 = bf16[1,1,2,32,5120]{4,3,2,1,0:T(8,128)(2,1)S(1)} copy-done((bf16[1,1,2,32,5120]{4,3,2,1,0:T(8,128)(2,1)S(1)}, bf16[1,1,2,32,5120]{4,3,2,1,0:T(8,128)(2,1)}, u32[]{:S(2)}) %copy-start.2) | copy-done | bytes 655384
  3.9 0.0 copy-start.3
  3.9 1.1 %copy-done.3 = bf16[1,1,2,32,5120]{4,3,2,1,0:T(8,128)(2,1)S(1)} copy-done((bf16[1,1,2,32,5120]{4,3,2,1,0:T(8,128)(2,1)S(1)}, bf16[1,1,2,32,5120]{4,3,2,1,0:T(8,128)(2,1)}, u32[]{:S(2)}) %copy-start.3) | copy-done | bytes 655384
  5.0 0.0 copy-start.4
  5.0 0.7 copy-done.4
  5.7 93.7 %window_backward.1 = (bf16[1,1,2,32,5120]{4,3,2,1,0:T(8,128)(2,1)S(1)}, bf16[1,1,2,32,5120]{4,3,2,1,0:T(8,128)(2,1)S(1)}, bf16[1,1,2,32,5120]{4,3,2,1,0:T(8,128)(2,1)S(1)}) custom-call(bf16[1,1,2,32,5120]{4,3,2,1,0:T(8,128)(2,1)S(1)} %copy-done, bf16[1,1,2,32,5120]{4,3,2,1,0:T(8,128)(2,1)S(1)} %copy-done.1, bf16[1,1,2,32,5120]{4,3,2,1,0:T(8,128)(2,1)S(1)} %copy-done.2, ...), custom_call_target="tpu_custom_call" | custom-call | flops 5033164800 | bytes 4587520 | tf_op jit(solution)/shard_map/window_backward/pallas_call | solution.py:257
  99.4 0.8 copy.11
  100.2 0.8 copy.12
  101.1 0.8 copy.13
Async XLA Ops:
  0.6 1.1 %copy-start = (bf16[1,1,2,32,5120]{4,3,2,1,0:T(8,128)(2,1)S(1)}, bf16[1,1,2,32,5120]{4,3,2,1,0:T(8,128)(2,1)}, u32[]{:S(2)}) copy-start(bf16[1,1,2,32,5120]{4,3,2,1,0:T(8,128)(2,1)} %q_ref.1) | copy-start | bytes 1966084
  1.7 1.1 %copy-start.1 = (bf16[1,1,2,32,5120]{4,3,2,1,0:T(8,128)(2,1)S(1)}, bf16[1,1,2,32,5120]{4,3,2,1,0:T(8,128)(2,1)}, u32[]{:S(2)}) copy-start(bf16[1,1,2,32,5120]{4,3,2,1,0:T(8,128)(2,1)} %k_ref.1) | copy-start | bytes 1966084
  2.8 1.1 %copy-start.2 = (bf16[1,1,2,32,5120]{4,3,2,1,0:T(8,128)(2,1)S(1)}, bf16[1,1,2,32,5120]{4,3,2,1,0:T(8,128)(2,1)}, u32[]{:S(2)}) copy-start(bf16[1,1,2,32,5120]{4,3,2,1,0:T(8,128)(2,1)} %v_ref.1) | copy-start | bytes 1966084
  3.9 1.1 %copy-start.3 = (bf16[1,1,2,32,5120]{4,3,2,1,0:T(8,128)(2,1)S(1)}, bf16[1,1,2,32,5120]{4,3,2,1,0:T(8,128)(2,1)}, u32[]{:S(2)}) copy-start(bf16[1,1,2,32,5120]{4,3,2,1,0:T(8,128)(2,1)} %g_ref.1) | copy-start | bytes 1966084
  5.0 0.7 copy-start.4

commit v2 on v1

--- a/solution.py
+++ b/solution.py
@@ -22,7 +22,7 @@
     return lax.dot_general(a, b, dims, preferred_element_type=jnp.float32)
 
 
-def phase_a(j, p, qg, kv, bias, es, dps, ms, pst):
+def phase_a(first, last, j, p, qg, kv, bias, es, dps, ms, pst):
     scale = LOG2E * HD**-0.5
 
     def block(i, carry):
@@ -51,7 +51,7 @@
         pst[j, s, f, 2:3, :] = sum(w * d for w, d in zip(ws, prods))
         return carry
 
-    lax.fori_loop(0, 6, block, 0)
+    lax.fori_loop(first, last, block, 0)
 
 
 def combine(j, pst, prc, fin):
@@ -65,7 +65,7 @@
         fin[j, 1, f, 1:2, :] = prod / total
 
 
-def phase_b(j, p, qg, kv, es, dps, ms, fin, dka, dva, dqs, dqf, ost):
+def phase_b(first, last, j, p, qg, kv, es, dps, ms, fin, dka, dva, dqs, dqf, ost):
     scale = HD**-0.5
     dka[...] = jnp.zeros_like(dka)
     dva[...] = jnp.zeros_like(dva)
@@ -95,30 +95,39 @@
 
         return carry
 
-    lax.fori_loop(0, 6, block, 0)
+    lax.fori_loop(first, last, block, 0)
     ost[j, 1] = (dka[...] * scale).astype(jnp.bfloat16).reshape(ost.shape[2:])
     ost[j, 2] = dva[...].astype(jnp.bfloat16).reshape(ost.shape[2:])
 
 
-def kernel(nh, q_ref, k_ref, v_ref, g_ref, nb_ref, oq_ref, ok_ref, ov_ref,
-           qg, kv, tab, bias, es, dps, ms, pst, prc, fin, dka, dva, dqs, dqr, dqf, ost,
+def kernel(nh, q_ref, k_ref, v_ref, g_ref, nb_hbm, oq_ref, ok_ref, ov_ref,
+           nb_ref, qg, kv, tab, bias, es, dps, ms, pst, prc, fin, dka, dva, dqs, dqr, dqf, ost,
            xin_s, xin_r, halo_s, halo_r, part_s, part_r, fin_s, fin_r, dq_s, dq_r, out_s, out_r,
-           tab_s, tab_r, bias_s, bias_r):
+           tab_s, tab_r, bias_s, bias_r, nb_s):
     f = lax.axis_index("frames")
     h = lax.axis_index("rows")
     x = lax.axis_index("heads")
     me = x * 2 + f
-    up, down = lax.rem(h + NROWS - 1, NROWS), lax.rem(h + 1, NROWS)
-    beside = (f, up, x), (f, down, x)
+    beside = (f, jnp.maximum(h - 1, 0), x), (f, jnp.minimum(h + 1, NROWS - 1), x)
+    held = h > 0, h < NROWS - 1
+    first, last = jnp.where(held[0], 0, 2), jnp.where(held[1], 6, 4)
 
     def member(k):
         other = lax.rem(me + k, 8)
         return other, (other % 2, h, other // 2)
 
+    near = pltpu.make_async_copy(nb_hbm, nb_ref, nb_s)
+    near.start()
     barrier = pltpu.get_barrier_semaphore()
-    for device in [member(k)[1] for k in range(1, 8)] + list(beside):
-        pl.semaphore_signal(barrier, inc=1, device_id=device, device_id_type=MESH)
-    pl.semaphore_wait(barrier, 9)
+    for k in range(1, 8):
+        pl.semaphore_signal(barrier, inc=1, device_id=member(k)[1], device_id_type=MESH)
+    for n in range(2):
+
+        @pl.when(held[n])
+        def _():
+            pl.semaphore_signal(barrier, inc=1, device_id=beside[n], device_id_type=MESH)
+
+    pl.semaphore_wait(barrier, 7 + held[0].astype(jnp.int32) + held[1].astype(jnp.int32))
 
     def remote(src, dst, send, recv, device):
         return pltpu.make_async_remote_copy(
@@ -127,6 +136,10 @@
 
     def await_bytes(ref, sem):
         pltpu.make_async_copy(ref, ref, sem).wait()
+
+    def each(action):
+        for n in range(2):
+            pl.when(held[n])(functools.partial(action, n))
 
     def lanes(owner, j):
         return pl.ds(pl.multiple_of((owner * nh + j) * HD, HD), HD)
@@ -148,8 +161,14 @@
             other, device = member(k)
             remote(ost.at[j, a, other % 2, :, other // 2], to, out_s.at[j, a], out_r.at[a], device).start()
 
+    def blank(n):
+        dqr[:, n] = jnp.zeros_like(dqr[:, n])
+        prc[:, n, :, 0:1, :] = jnp.full_like(prc[:, n, :, 0:1, :], NONE)
+        prc[:, n, :, 1:8, :] = jnp.zeros_like(prc[:, n, :, 1:8, :])
+
     lax.fori_loop(0, nh, lambda j, c: (enter(j), c)[1], 0)
 
+    near.wait()
     for n, dr in enumerate((1, 0, -1)):
         row = h + dr
         inside = jnp.logical_and(row >= 0, row < NROWS)
@@ -165,25 +184,29 @@
     swap.wait()
     bias[1] = tab[1]
     lend = [remote(tab.at[2 * n], bias.at[2 * n], bias_s.at[n], bias_r.at[n], beside[1 - n]) for n in range(2)]
-    for copy in lend:
-        copy.start()
+    each(lambda n: lend[1 - n].start())
+
+    @pl.when(h == 0)
+    def _():
+        blank(0)
+
+    @pl.when(h == NROWS - 1)
+    def _():
+        blank(1)
 
     def step(t, carry):
         @pl.when(t < nh)
         def _():
             j = t
             await_bytes(qg.at[1, j], xin_r.at[j, 0])
-            for n in range(2):
-                remote(qg.at[1, j], qg.at[2 * n, j], halo_s.at[n, j], halo_r.at[n, j], beside[1 - n]).start()
+            each(lambda n: remote(qg.at[1, j], qg.at[2 - 2 * n, j], halo_s.at[n, j], halo_r.at[1 - n, j], beside[n]).start())
 
         @pl.when(jnp.logical_and(t >= 2, t < nh + 2))
         def _():
             j = t - 2
-            for n in range(2):
-                await_bytes(prc.at[j, n], part_r.at[n, j])
+            each(lambda n: await_bytes(prc.at[j, n], part_r.at[n, j]))
             combine(j, pst, prc, fin)
-            for n in range(2):
-                remote(fin.at[j, 1], fin.at[j, 2 * n], fin_s.at[n, j], fin_r.at[n, j], beside[1 - n]).start()
+            each(lambda n: remote(fin.at[j, 1], fin.at[j, 2 - 2 * n], fin_s.at[n, j], fin_r.at[1 - n, j], beside[n]).start())
 
         @pl.when(jnp.logical_and(t >= 1, t < nh + 1))
         def _():
@@ -191,44 +214,37 @@
 
             @pl.when(t == 1)
             def _():
-                for copy in lend:
-                    copy.wait_recv()
+                each(lambda n: lend[n].wait_recv())
 
             await_bytes(kv.at[j], xin_r.at[j, 1])
-            for n in range(2):
-                await_bytes(qg.at[2 * n, j], halo_r.at[n, j])
-            phase_a(j, j % 2, qg, kv, bias, es, dps, ms, pst)
-            for n in range(2):
-                remote(pst.at[j, 2 * n], prc.at[j, 1 - n], part_s.at[n, j], part_r.at[1 - n, j], beside[n]).start()
-
-        @pl.when(jnp.logical_and(t >= 2, t < nh + 2))
-        def _():
-            j = t - 2
-            for n in range(2):
-                await_bytes(fin.at[j, 2 * n], fin_r.at[n, j])
-            phase_b(j, j % 2, qg, kv, es, dps, ms, fin, dka, dva, dqs, dqf, ost)
-            for n in range(2):
-                remote(dqs.at[j, 2 * n], dqr.at[j, 1 - n], dq_s.at[n, j], dq_r.at[1 - n, j], beside[n]).start()
+            each(lambda n: await_bytes(qg.at[2 * n, j], halo_r.at[n, j]))
+            phase_a(first, last, j, lax.rem(j, 3), qg, kv, bias, es, dps, ms, pst)
+            each(lambda n: remote(pst.at[j, 2 * n], prc.at[j, 1 - n], part_s.at[n, j], part_r.at[1 - n, j], beside[n]).start())
+
+        @pl.when(jnp.logical_and(t >= 3, t < nh + 3))
+        def _():
+            j = t - 3
+            each(lambda n: await_bytes(fin.at[j, 2 * n], fin_r.at[n, j]))
+            phase_b(first, last, j, lax.rem(j, 3), qg, kv, es, dps, ms, fin, dka, dva, dqs, dqf, ost)
+            each(lambda n: remote(dqs.at[j, 2 * n], dqr.at[j, 1 - n], dq_s.at[n, j], dq_r.at[1 - n, j], beside[n]).start())
             leave(j, 1, ok_ref)
             leave(j, 2, ov_ref)
 
-        @pl.when(t >= 3)
-        def _():
-            j = t - 3
-            for n in range(2):
-                await_bytes(dqr.at[j, n], dq_r.at[n, j])
+        @pl.when(t >= 5)
+        def _():
+            j = t - 5
+            each(lambda n: await_bytes(dqr.at[j, n], dq_r.at[n, j]))
             total = dqf[j] + dqr[j, 0].astype(jnp.float32) + dqr[j, 1].astype(jnp.float32)
             ost[j, 0] = total.astype(jnp.bfloat16).reshape(ost.shape[2:])
             leave(j, 0, oq_ref)
 
         return carry
 
-    lax.fori_loop(0, nh + 3, step, 0)
+    lax.fori_loop(0, nh + 5, step, 0)
 
     for a, out in enumerate((oq_ref, ok_ref, ov_ref)):
         await_bytes(out, out_r.at[a])
-    for copy in lend:
-        copy.wait_send()
+    each(lambda n: lend[1 - n].wait_send())
 
     def settle(j, carry):
         sent = dqs.at[j, 0, pl.ds(0, 7 * TILE // 2)]
@@ -236,14 +252,29 @@
             await_bytes(sent, xin_s.at[j, a])
         for a in range(3):
             await_bytes(sent, out_s.at[j, a])
-        for n in range(2):
+
+        def lent(n):
             await_bytes(qg.at[1, j], halo_s.at[n, j])
             await_bytes(prc.at[j, n], part_s.at[n, j])
             await_bytes(prc.at[j, n], fin_s.at[n, j])
             await_bytes(dqr.at[j, n], dq_s.at[n, j])
+
+        each(lent)
         return carry
 
     lax.fori_loop(0, nh, settle, 0)
+
+
+def hand_over(aq, ak, av, bq, bk, bv, room, into, out):
+    ins = [pltpu.make_async_copy(a, room.at[n], into.at[n]) for n, a in enumerate((aq, ak, av))]
+    outs = [pltpu.make_async_copy(room.at[n], b, out.at[n]) for n, b in enumerate((bq, bk, bv))]
+    for copy in ins:
+        copy.start()
+    for arrived, copy in zip(ins, outs):
+        arrived.wait()
+        copy.start()
+    for copy in outs:
+        copy.wait()
 
 
 def local(queries, keys, values, out_grad, neighbours):
@@ -254,19 +285,20 @@
     any_spec = pl.BlockSpec(memory_space=pl.ANY)
     shape = jax.ShapeDtypeStruct(queries.shape, bf)
     products = 5 * 512 * 1536 * HD * nh
-    return pl.pallas_call(
+    grads = pl.pallas_call(
         functools.partial(kernel, nh),
         out_shape=(shape, shape, shape),
-        in_specs=[any_spec] * 4 + [pl.BlockSpec(memory_space=pltpu.VMEM)],
+        in_specs=[any_spec] * 5,
         out_specs=[any_spec] * 3,
         scratch_shapes=[
+            pltpu.VMEM(neighbours.shape, jnp.int32),
             pltpu.VMEM((3, nh, 2) + tiles, bf),
             pltpu.VMEM((nh, 2) + tiles, bf),
             pltpu.VMEM((3, 2, 8, 256), f32),
             pltpu.VMEM((3, 2, 8, 256), f32),
-            pltpu.VMEM((2, 6, 4, TILE, 256), f32),
-            pltpu.VMEM((2, 6, 4, TILE, 256), f32),
-            pltpu.VMEM((2, 6, 8, 256), f32),
+            pltpu.VMEM((3, 6, 4, TILE, 256), f32),
+            pltpu.VMEM((3, 6, 4, TILE, 256), f32),
+            pltpu.VMEM((3, 6, 8, 256), f32),
             pltpu.VMEM((nh, 3, 2, 8, 256), f32),
             pltpu.VMEM((nh, 2, 2, 8, 256), f32),
             pltpu.VMEM((nh, 3, 2, 8, 256), f32),
@@ -284,15 +316,25 @@
             dma((nh, 3)), dma((3,)),
             dma(()), dma(()),
             dma((2,)), dma((2,)),
+            dma(()),
         ],
         compiler_params=pltpu.CompilerParams(
-            collective_id=0, has_side_effects=True, vmem_limit_bytes=48 * 1024 * 1024
+            collective_id=0, has_side_effects=True, vmem_limit_bytes=60 * 1024 * 1024
         ),
         cost_estimate=pl.CostEstimate(
             flops=2 * products, bytes_accessed=7 * 2 * queries.size, transcendentals=512 * 1536 * nh
         ),
         name="window_backward",
     )(queries, keys, values, out_grad, neighbours)
+    return pl.pallas_call(
+        hand_over,
+        out_shape=(shape, shape, shape),
+        in_specs=[any_spec] * 3,
+        out_specs=[any_spec] * 3,
+        scratch_shapes=[pltpu.VMEM((3,) + queries.shape, bf), dma((3,)), dma((3,))],
+        compiler_params=pltpu.CompilerParams(vmem_limit_bytes=60 * 1024 * 1024),
+        name="hand_over",
+    )(*grads)
 
 
 def solution(mesh):

time: 102 us -> 76.6 us (0.75)
  the two profiles are of different devices: /device:TPU:1 before, /device:TPU:97 now
where the time goes in v2:
time: 76.6 us; the launch traced here: 76.5 us
  Pallas kernels  75.9 us (99%)
    pallas_call x1, Pallas kernels, local(): pl.pallas_call(functools.partial(kernel, nh), out_shape=(shape, shape, sh...  73.4 us
    pallas_call x1, Pallas kernels, local(): pl.pallas_call(hand_over, out_shape=(shape, shape, shape), in_specs=[any_...  2.41 us

profile of v2, /device:TPU:97, one launch (start us, length us, event | category | flops | bytes accessed | tf_op | source)
XLA Modules:
  0.0 76.5 jit_solution(4448173995779106586)
XLA Ops:
  0.6 73.4 %window_backward.1 = (bf16[1,1,2,32,5120]{4,3,2,1,0:T(8,128)(2,1)}, bf16[1,1,2,32,5120]{4,3,2,1,0:T(8,128)(2,1)}, bf16[1,1,2,32,5120]{4,3,2,1,0:T(8,128)(2,1)}) custom-call(bf16[1,1,2,32,5120]{4,3,2,1,0:T(8,128)(2,1)} %q_ref.1, bf16[1,1,2,32,5120]{4,3,2,1,0:T(8,128)(2,1)} %k_ref.1, bf16[1,1,2,32,5120]{4,3,2,1,0:T(8,128)(2,1)} %v_ref.1, ...), custom_call_target="tpu_custom_call" | custom-call | flops 5033164800 | bytes 4587520 | tf_op jit(solution)/shard_map/window_backward/pallas_call | solution.py:288
  74.1 2.4 %hand_over.1 = (bf16[1,1,2,32,5120]{4,3,2,1,0:T(8,128)(2,1)}, bf16[1,1,2,32,5120]{4,3,2,1,0:T(8,128)(2,1)}, bf16[1,1,2,32,5120]{4,3,2,1,0:T(8,128)(2,1)}) custom-call(bf16[1,1,2,32,5120]{4,3,2,1,0:T(8,128)(2,1)} %get-tuple-element.6.aq, bf16[1,1,2,32,5120]{4,3,2,1,0:T(8,128)(2,1)} %get-tuple-element.7.ak, bf16[1,1,2,32,5120]{4,3,2,1,0:T(8,128)(2,1)} %get-tuple-element.8.av), custom_call_target="tpu_custom_call" | custom-call | tf_op jit(solution)/shard_map/hand_over/pallas_call | solution.py:329

commit v3 on v2

--- a/solution.py
+++ b/solution.py
@@ -22,11 +22,11 @@
     return lax.dot_general(a, b, dims, preferred_element_type=jnp.float32)
 
 
-def phase_a(first, last, j, p, qg, kv, bias, es, dps, ms, pst):
+def phase_a(s, j, p, qg, kv, bias, es, dps, ms, pst):
     scale = LOG2E * HD**-0.5
 
-    def block(i, carry):
-        s, f = i // 2, i % 2
+    def block(f, carry):
+        i = 2 * s + f
         q = qg[s, j, 0, f].reshape(2 * TILE, HD)
         g = qg[s, j, 1, f].reshape(2 * TILE, HD)
         peaks, sums, prods = [], [], []
@@ -51,7 +51,7 @@
         pst[j, s, f, 2:3, :] = sum(w * d for w, d in zip(ws, prods))
         return carry
 
-    lax.fori_loop(first, last, block, 0)
+    lax.fori_loop(0, 2, block, 0)
 
 
 def combine(j, pst, prc, fin):
@@ -65,13 +65,11 @@
         fin[j, 1, f, 1:2, :] = prod / total
 
 
-def phase_b(first, last, j, p, qg, kv, es, dps, ms, fin, dka, dva, dqs, dqf, ost):
+def phase_b(s, j, p, qg, kv, es, dps, ms, fin, dka, dva, dqs, dqf):
     scale = HD**-0.5
-    dka[...] = jnp.zeros_like(dka)
-    dva[...] = jnp.zeros_like(dva)
-
-    def block(i, carry):
-        s, f = i // 2, i % 2
+
+    def block(f, carry):
+        i = 2 * s + f
         q = qg[s, j, 0, f].reshape(2 * TILE, HD)
         g = qg[s, j, 1, f].reshape(2 * TILE, HD)
         lse = fin[j, s, f, 0:1, :]
@@ -87,17 +85,13 @@
             dq += dot(ds, k, TN)
         dq = dq * scale
         rows = pl.ds(pl.multiple_of(f * 2 * TILE, 2 * TILE), 2 * TILE)
-        dqs[j, s, rows] = dq.astype(jnp.bfloat16)
-
-        @pl.when(s == 1)
-        def _():
+        if isinstance(s, int):
             dqf[j, rows] = dq
-
-        return carry
-
-    lax.fori_loop(first, last, block, 0)
-    ost[j, 1] = (dka[...] * scale).astype(jnp.bfloat16).reshape(ost.shape[2:])
-    ost[j, 2] = dva[...].astype(jnp.bfloat16).reshape(ost.shape[2:])
+        else:
+            dqs[j, s, rows] = dq.astype(jnp.bfloat16)
+        return carry
+
+    lax.fori_loop(0, 2, block, 0)
 
 
 def kernel(nh, q_ref, k_ref, v_ref, g_ref, nb_hbm, oq_ref, ok_ref, ov_ref,
@@ -110,7 +104,6 @@
     me = x * 2 + f
     beside = (f, jnp.maximum(h - 1, 0), x), (f, jnp.minimum(h + 1, NROWS - 1), x)
     held = h > 0, h < NROWS - 1
-    first, last = jnp.where(held[0], 0, 2), jnp.where(held[1], 6, 4)
 
     def member(k):
         other = lax.rem(me + k, 8)
@@ -144,15 +137,15 @@
     def lanes(owner, j):
         return pl.ds(pl.multiple_of((owner * nh + j) * HD, HD), HD)
 
-    def enter(j):
-        for a, (src, dst) in enumerate(((q_ref, qg.at[1, j, 0]), (g_ref, qg.at[1, j, 1]),
-                                        (k_ref, kv.at[j, 0]), (v_ref, kv.at[j, 1]))):
+    def enter(j, pair):
+        sides = ((q_ref, qg.at[1, j, 0]), (g_ref, qg.at[1, j, 1])), ((k_ref, kv.at[j, 0]), (v_ref, kv.at[j, 1]))
+        for a, (src, dst) in enumerate(sides[pair]):
             to = dst.at[f, :, x]
-            recv = xin_r.at[j, a // 2]
+            recv = xin_r.at[j, 2 * pair + a]
             pltpu.make_async_copy(src.at[0, 0, :, :, lanes(me, j)], to, recv).start()
             for k in range(1, 8):
                 other, device = member(k)
-                remote(src.at[0, 0, :, :, lanes(other, j)], to, xin_s.at[j, a], recv, device).start()
+                remote(src.at[0, 0, :, :, lanes(other, j)], to, xin_s.at[j, 2 * pair + a], recv, device).start()
 
     def leave(j, a, out):
         to = out.at[0, 0, :, :, lanes(me, j)]
@@ -166,7 +159,13 @@
         prc[:, n, :, 0:1, :] = jnp.full_like(prc[:, n, :, 0:1, :], NONE)
         prc[:, n, :, 1:8, :] = jnp.zeros_like(prc[:, n, :, 1:8, :])
 
-    lax.fori_loop(0, nh, lambda j, c: (enter(j), c)[1], 0)
+    def enter_both(j, carry):
+        pl.when(j < nh)(lambda: enter(j, 0))
+        pl.when(j >= 1)(lambda: enter(j - 1, 1))
+        return carry
+
+    enter(0, 0)
+    lax.fori_loop(1, nh + 1, enter_both, 0)
 
     near.wait()
     for n, dr in enumerate((1, 0, -1)):
@@ -194,53 +193,89 @@
     def _():
         blank(1)
 
+    def lend_queries(j):
+        for a in range(2):
+            await_bytes(qg.at[1, j, a], xin_r.at[j, a])
+            each(lambda n: remote(qg.at[1, j, a], qg.at[2 - 2 * n, j, a], halo_s.at[n, j], halo_r.at[1 - n, j], beside[n]).start())
+
+    def return_queries(j):
+        each(lambda n: remote(dqs.at[j, 2 * n], dqr.at[j, 1 - n], dq_s.at[n, j], dq_r.at[1 - n, j], beside[n]).start())
+
+    def finish_queries(j):
+        each(lambda n: await_bytes(dqr.at[j, n], dq_r.at[n, j]))
+        total = dqf[j] + dqr[j, 0].astype(jnp.float32) + dqr[j, 1].astype(jnp.float32)
+        ost[j, 0] = total.astype(jnp.bfloat16).reshape(ost.shape[2:])
+        leave(j, 0, oq_ref)
+
+    def neighbours_of(action):
+        def body(n, carry):
+            ahead = jnp.where(n == 0, h - 1, h + 1)
+            pl.when(jnp.logical_and(ahead >= 0, ahead < NROWS))(lambda: action(n, (f, ahead, x)))
+            return carry
+
+        lax.fori_loop(0, 2, body, 0)
+
+    def weights_beside(j):
+        def one(n, device):
+            await_bytes(qg.at[2 * n, j], halo_r.at[n, j])
+            phase_a(2 * n, j, lax.rem(j, 3), qg, kv, bias, es, dps, ms, pst)
+            remote(pst.at[j, 2 * n], prc.at[j, 1 - n], part_s.at[n, j], part_r.at[1 - n, j], device).start()
+
+        neighbours_of(one)
+
+    def gradients(j):
+        dka[...] = jnp.zeros_like(dka)
+        dva[...] = jnp.zeros_like(dva)
+
+        def one(n, device):
+            await_bytes(fin.at[j, 2 * n], fin_r.at[n, j])
+            phase_b(2 * n, j, lax.rem(j, 3), qg, kv, es, dps, ms, fin, dka, dva, dqs, dqf)
+
+        neighbours_of(one)
+        pl.when(j == nh - 1)(lambda: return_queries(j))
+        phase_b(1, j, lax.rem(j, 3), qg, kv, es, dps, ms, fin, dka, dva, dqs, dqf)
+        ost[j, 1] = (dka[...] * HD**-0.5).astype(jnp.bfloat16).reshape(ost.shape[2:])
+        ost[j, 2] = dva[...].astype(jnp.bfloat16).reshape(ost.shape[2:])
+        leave(j, 1, ok_ref)
+        leave(j, 2, ov_ref)
+
     def step(t, carry):
+        @pl.when(t + 1 < nh)
+        def _():
+            lend_queries(t + 1)
+
+        pl.when(t == nh - 2)(lambda: return_queries(0))
+
         @pl.when(t < nh)
         def _():
-            j = t
-            await_bytes(qg.at[1, j], xin_r.at[j, 0])
-            each(lambda n: remote(qg.at[1, j], qg.at[2 - 2 * n, j], halo_s.at[n, j], halo_r.at[1 - n, j], beside[n]).start())
-
-        @pl.when(jnp.logical_and(t >= 2, t < nh + 2))
-        def _():
-            j = t - 2
+            @pl.when(t == 0)
+            def _():
+                each(lambda n: lend[n].wait_recv())
+
+            for a in range(2):
+                await_bytes(kv.at[t, a], xin_r.at[t, 2 + a])
+            phase_a(1, t, lax.rem(t, 3), qg, kv, bias, es, dps, ms, pst)
+            weights_beside(t)
+
+        @pl.when(jnp.logical_and(t >= 1, t < nh + 1))
+        def _():
+            j = t - 1
             each(lambda n: await_bytes(prc.at[j, n], part_r.at[n, j]))
             combine(j, pst, prc, fin)
             each(lambda n: remote(fin.at[j, 1], fin.at[j, 2 - 2 * n], fin_s.at[n, j], fin_r.at[1 - n, j], beside[n]).start())
 
-        @pl.when(jnp.logical_and(t >= 1, t < nh + 1))
-        def _():
-            j = t - 1
-
-            @pl.when(t == 1)
-            def _():
-                each(lambda n: lend[n].wait_recv())
-
-            await_bytes(kv.at[j], xin_r.at[j, 1])
-            each(lambda n: await_bytes(qg.at[2 * n, j], halo_r.at[n, j]))
-            phase_a(first, last, j, lax.rem(j, 3), qg, kv, bias, es, dps, ms, pst)
-            each(lambda n: remote(pst.at[j, 2 * n], prc.at[j, 1 - n], part_s.at[n, j], part_r.at[1 - n, j], beside[n]).start())
-
-        @pl.when(jnp.logical_and(t >= 3, t < nh + 3))
-        def _():
-            j = t - 3
-            each(lambda n: await_bytes(fin.at[j, 2 * n], fin_r.at[n, j]))
-            phase_b(first, last, j, lax.rem(j, 3), qg, kv, es, dps, ms, fin, dka, dva, dqs, dqf, ost)
-            each(lambda n: remote(dqs.at[j, 2 * n], dqr.at[j, 1 - n], dq_s.at[n, j], dq_r.at[1 - n, j], beside[n]).start())
-            leave(j, 1, ok_ref)
-            leave(j, 2, ov_ref)
-
-        @pl.when(t >= 5)
-        def _():
-            j = t - 5
-            each(lambda n: await_bytes(dqr.at[j, n], dq_r.at[n, j]))
-            total = dqf[j] + dqr[j, 0].astype(jnp.float32) + dqr[j, 1].astype(jnp.float32)
-            ost[j, 0] = total.astype(jnp.bfloat16).reshape(ost.shape[2:])
-            leave(j, 0, oq_ref)
-
-        return carry
-
-    lax.fori_loop(0, nh + 5, step, 0)
+        pl.when(t >= nh - 1)(lambda: return_queries(t - nh + 2))
+
+        @pl.when(t >= 2)
+        def _():
+            gradients(t - 2)
+
+        pl.when(t == nh)(lambda: finish_queries(0))
+        return carry
+
+    lend_queries(0)
+    lax.fori_loop(0, nh + 2, step, 0)
+    lax.fori_loop(1, nh, lambda j, c: (finish_queries(j), c)[1], 0)
 
     for a, out in enumerate((oq_ref, ok_ref, ov_ref)):
         await_bytes(out, out_r.at[a])
@@ -266,8 +301,9 @@
 
 
 def hand_over(aq, ak, av, bq, bk, bv, room, into, out):
-    ins = [pltpu.make_async_copy(a, room.at[n], into.at[n]) for n, a in enumerate((aq, ak, av))]
-    outs = [pltpu.make_async_copy(room.at[n], b, out.at[n]) for n, b in enumerate((bq, bk, bv))]
+    pieces = [(n, c, a.at[0, 0, c], b.at[0, 0, c]) for n, (a, b) in enumerate(((aq, bq), (ak, bk), (av, bv))) for c in range(2)]
+    ins = [pltpu.make_async_copy(a, room.at[n, c], into.at[n, c]) for n, c, a, b in pieces]
+    outs = [pltpu.make_async_copy(room.at[n, c], b, out.at[n, c]) for n, c, a, b in pieces]
     for copy in ins:
         copy.start()
     for arrived, copy in zip(ins, outs):
@@ -308,7 +344,7 @@
             pltpu.VMEM((nh, 2, 512, HD), bf),
             pltpu.VMEM((nh, 512, HD), f32),
             pltpu.VMEM((nh, 3) + tiles, bf),
-            dma((nh, 4)), dma((nh, 2)),
+            dma((nh, 4)), dma((nh, 4)),
             dma((2, nh)), dma((2, nh)),
             dma((2, nh)), dma((2, nh)),
             dma((2, nh)), dma((2, nh)),
@@ -331,7 +367,7 @@
         out_shape=(shape, shape, shape),
         in_specs=[any_spec] * 3,
         out_specs=[any_spec] * 3,
-        scratch_shapes=[pltpu.VMEM((3,) + queries.shape, bf), dma((3,)), dma((3,))],
+        scratch_shapes=[pltpu.VMEM((3,) + queries.shape[2:], bf), dma((3, 2)), dma((3, 2))],
         compiler_params=pltpu.CompilerParams(vmem_limit_bytes=60 * 1024 * 1024),
         name="hand_over",
     )(*grads)

time: 76.6 us -> 70.3 us (0.918)
  Pallas kernels: 75.9 us -> 69.5 us
    pallas_call x1, Pallas kernels: 73.4 us -> 67.2 us  [local(): pl.pallas_call(functools.partial(kernel, nh), out_shape=(shape, shape, sh...]
where the time goes in v3:
time: 70.3 us; the launch traced here: 70.1 us
  Pallas kernels  69.5 us (99%)
    pallas_call x1, Pallas kernels, local(): pl.pallas_call(functools.partial(kernel, nh), out_shape=(shape, shape, sh...  67.2 us
    pallas_call x1, Pallas kernels, local(): pl.pallas_call(hand_over, out_shape=(shape, shape, shape), in_specs=[any_...  2.34 us

profile of v3, /device:TPU:97, one launch (start us, length us, event | category | flops | bytes accessed | tf_op | source)
XLA Modules:
  0.0 70.1 jit_solution(12078710332166199565)
XLA Ops:
  0.6 67.2 %window_backward.1 = (bf16[1,1,2,32,5120]{4,3,2,1,0:T(8,128)(2,1)}, bf16[1,1,2,32,5120]{4,3,2,1,0:T(8,128)(2,1)}, bf16[1,1,2,32,5120]{4,3,2,1,0:T(8,128)(2,1)}) custom-call(bf16[1,1,2,32,5120]{4,3,2,1,0:T(8,128)(2,1)} %q_ref.1, bf16[1,1,2,32,5120]{4,3,2,1,0:T(8,128)(2,1)} %k_ref.1, bf16[1,1,2,32,5120]{4,3,2,1,0:T(8,128)(2,1)} %v_ref.1, ...), custom_call_target="tpu_custom_call" | custom-call | flops 5033164800 | bytes 4587520 | tf_op jit(solution)/shard_map/window_backward/pallas_call | solution.py:324
  67.8 2.3 %hand_over.1 = (bf16[1,1,2,32,5120]{4,3,2,1,0:T(8,128)(2,1)}, bf16[1,1,2,32,5120]{4,3,2,1,0:T(8,128)(2,1)}, bf16[1,1,2,32,5120]{4,3,2,1,0:T(8,128)(2,1)}) custom-call(bf16[1,1,2,32,5120]{4,3,2,1,0:T(8,128)(2,1)} %get-tuple-element.6.aq, bf16[1,1,2,32,5120]{4,3,2,1,0:T(8,128)(2,1)} %get-tuple-element.7.ak, bf16[1,1,2,32,5120]{4,3,2,1,0:T(8,128)(2,1)} %get-tuple-element.8.av), custom_call_target="tpu_custom_call" | custom-call | tf_op jit(solution)/shard_map/hand_over/pallas_call | solution.py:365

commit v4 on v3

--- a/solution.py
+++ b/solution.py
@@ -51,7 +51,8 @@
         pst[j, s, f, 2:3, :] = sum(w * d for w, d in zip(ws, prods))
         return carry
 
-    lax.fori_loop(0, 2, block, 0)
+    block(0, 0)
+    block(1, 0)
 
 
 def combine(j, pst, prc, fin):
@@ -74,16 +75,17 @@
         g = qg[s, j, 1, f].reshape(2 * TILE, HD)
         lse = fin[j, s, f, 0:1, :]
         delta = fin[j, s, f, 1:2, :]
-        dq = jnp.zeros((2 * TILE, HD), jnp.float32)
+        probs, grads = [], []
         for kt in range(4):
-            k = kv[j, 0, kt // 2, kt % 2].reshape(TILE, HD)
             r = jnp.exp2(ms[p, i, kt : kt + 1, :] - lse)
             prob = es[p, i, kt] * r
             ds = (prob * (dps[p, i, kt] - delta)).astype(jnp.bfloat16)
-            dva[kt] += dot(prob.astype(jnp.bfloat16), g, NN)
-            dka[kt] += dot(ds, q, NN)
-            dq += dot(ds, k, TN)
-        dq = dq * scale
+            probs.append(prob.astype(jnp.bfloat16))
+            grads.append(ds)
+        probs, grads = jnp.concatenate(probs), jnp.concatenate(grads)
+        dva[...] += dot(probs, g, NN).reshape(dva.shape)
+        dka[...] += dot(grads, q, NN).reshape(dka.shape)
+        dq = dot(kv[j, 0].reshape(4 * TILE, HD), grads, TN).T * scale
         rows = pl.ds(pl.multiple_of(f * 2 * TILE, 2 * TILE), 2 * TILE)
         if isinstance(s, int):
             dqf[j, rows] = dq
@@ -91,13 +93,14 @@
             dqs[j, s, rows] = dq.astype(jnp.bfloat16)
         return carry
 
-    lax.fori_loop(0, 2, block, 0)
+    block(0, 0)
+    block(1, 0)
 
 
 def kernel(nh, q_ref, k_ref, v_ref, g_ref, nb_hbm, oq_ref, ok_ref, ov_ref,
            nb_ref, qg, kv, tab, bias, es, dps, ms, pst, prc, fin, dka, dva, dqs, dqr, dqf, ost,
            xin_s, xin_r, halo_s, halo_r, part_s, part_r, fin_s, fin_r, dq_s, dq_r, out_s, out_r,
-           tab_s, tab_r, bias_s, bias_r, nb_s):
+           tab_s, tab_r, bias_s, bias_r, nb_s, dqh_s, dqh_r):
     f = lax.axis_index("frames")
     h = lax.axis_index("rows")
     x = lax.axis_index("heads")
@@ -119,53 +122,6 @@
         @pl.when(held[n])
         def _():
             pl.semaphore_signal(barrier, inc=1, device_id=beside[n], device_id_type=MESH)
-
-    pl.semaphore_wait(barrier, 7 + held[0].astype(jnp.int32) + held[1].astype(jnp.int32))
-
-    def remote(src, dst, send, recv, device):
-        return pltpu.make_async_remote_copy(
-            src_ref=src, dst_ref=dst, send_sem=send, recv_sem=recv, device_id=device, device_id_type=MESH
-        )
-
-    def await_bytes(ref, sem):
-        pltpu.make_async_copy(ref, ref, sem).wait()
-
-    def each(action):
-        for n in range(2):
-            pl.when(held[n])(functools.partial(action, n))
-
-    def lanes(owner, j):
-        return pl.ds(pl.multiple_of((owner * nh + j) * HD, HD), HD)
-
-    def enter(j, pair):
-        sides = ((q_ref, qg.at[1, j, 0]), (g_ref, qg.at[1, j, 1])), ((k_ref, kv.at[j, 0]), (v_ref, kv.at[j, 1]))
-        for a, (src, dst) in enumerate(sides[pair]):
-            to = dst.at[f, :, x]
-            recv = xin_r.at[j, 2 * pair + a]
-            pltpu.make_async_copy(src.at[0, 0, :, :, lanes(me, j)], to, recv).start()
-            for k in range(1, 8):
-                other, device = member(k)
-                remote(src.at[0, 0, :, :, lanes(other, j)], to, xin_s.at[j, 2 * pair + a], recv, device).start()
-
-    def leave(j, a, out):
-        to = out.at[0, 0, :, :, lanes(me, j)]
-        pltpu.make_async_copy(ost.at[j, a, f, :, x], to, out_r.at[a]).start()
-        for k in range(1, 8):
-            other, device = member(k)
-            remote(ost.at[j, a, other % 2, :, other // 2], to, out_s.at[j, a], out_r.at[a], device).start()
-
-    def blank(n):
-        dqr[:, n] = jnp.zeros_like(dqr[:, n])
-        prc[:, n, :, 0:1, :] = jnp.full_like(prc[:, n, :, 0:1, :], NONE)
-        prc[:, n, :, 1:8, :] = jnp.zeros_like(prc[:, n, :, 1:8, :])
-
-    def enter_both(j, carry):
-        pl.when(j < nh)(lambda: enter(j, 0))
-        pl.when(j >= 1)(lambda: enter(j - 1, 1))
-        return carry
-
-    enter(0, 0)
-    lax.fori_loop(1, nh + 1, enter_both, 0)
 
     near.wait()
     for n, dr in enumerate((1, 0, -1)):
@@ -178,20 +134,55 @@
                 found = jnp.max(found, axis=-1, keepdims=True)
                 tab[n, f, kt : kt + 1, c * TILE : (c + 1) * TILE] = jnp.broadcast_to(found, (1, TILE))
         tab[n, f, 4:8, :] = jnp.zeros((4, 2 * TILE), jnp.float32)
+
+    pl.semaphore_wait(barrier, 7 + held[0].astype(jnp.int32) + held[1].astype(jnp.int32))
+
+    def remote(src, dst, send, recv, device):
+        return pltpu.make_async_remote_copy(
+            src_ref=src, dst_ref=dst, send_sem=send, recv_sem=recv, device_id=device, device_id_type=MESH
+        )
+
+    def await_bytes(ref, sem):
+        pltpu.make_async_copy(ref, ref, sem).wait()
+
+    def each(action):
+        for n in range(2):
+            pl.when(held[n])(functools.partial(action, n))
+
+    def lanes(owner, j):
+        return pl.ds(pl.multiple_of((owner * nh + j) * HD, HD), HD)
+
+    def enter(j, pair):
+        sides = ((q_ref, qg.at[1, j, 0]), (g_ref, qg.at[1, j, 1])), ((k_ref, kv.at[j, 0]), (v_ref, kv.at[j, 1]))
+        for a, (src, dst) in enumerate(sides[pair]):
+            to = dst.at[f, :, x]
+            recv = xin_r.at[j, 2 * pair + a]
+            pltpu.make_async_copy(src.at[0, 0, :, :, lanes(me, j)], to, recv).start()
+            for k in range(1, 8):
+                other, device = member(k)
+                remote(src.at[0, 0, :, :, lanes(other, j)], to, xin_s.at[j, 2 * pair + a], recv, device).start()
+
+    def leave(j, a, out):
+        to = out.at[0, 0, :, :, lanes(me, j)]
+        pltpu.make_async_copy(ost.at[j, a, f, :, x], to, out_r.at[a]).start()
+        for k in range(1, 8):
+            other, device = member(k)
+            remote(ost.at[j, a, other % 2, :, other // 2], to, out_s.at[j, a], out_r.at[a], device).start()
+
+    def blank(n):
+        dqr[:, n] = jnp.zeros_like(dqr[:, n])
+        prc[:, n, :, 0:1, :] = jnp.full_like(prc[:, n, :, 0:1, :], NONE)
+        prc[:, n, :, 1:8, :] = jnp.zeros_like(prc[:, n, :, 1:8, :])
+
+    def enter_both(j, carry):
+        pl.when(j < nh)(lambda: enter(j, 0))
+        pl.when(j >= 1)(lambda: enter(j - 1, 1))
+        return carry
+
+    enter(0, 0)
     swap = remote(tab.at[:, f], tab.at[:, f], tab_s, tab_r, (1 - f, h, x))
     swap.start()
-    swap.wait()
-    bias[1] = tab[1]
-    lend = [remote(tab.at[2 * n], bias.at[2 * n], bias_s.at[n], bias_r.at[n], beside[1 - n]) for n in range(2)]
-    each(lambda n: lend[1 - n].start())
-
-    @pl.when(h == 0)
-    def _():
-        blank(0)
-
-    @pl.when(h == NROWS - 1)
-    def _():
-        blank(1)
+    lax.fori_loop(1, nh + 1, enter_both, 0)
 
     def lend_queries(j):
         for a in range(2):
@@ -200,6 +191,29 @@
 
     def return_queries(j):
         each(lambda n: remote(dqs.at[j, 2 * n], dqr.at[j, 1 - n], dq_s.at[n, j], dq_r.at[1 - n, j], beside[n]).start())
+
+    def return_half(half):
+        rows = pl.ds(half * 2 * TILE, 2 * TILE)
+        each(lambda n: remote(dqs.at[nh - 1, 2 * n, rows], dqr.at[nh - 1, 1 - n, rows], dqh_s.at[n, half], dqh_r.at[1 - n, half], beside[n]).start())
+
+    def finish_half(half):
+        j, rows = nh - 1, pl.ds(half * 2 * TILE, 2 * TILE)
+        each(lambda n: await_bytes(dqr.at[j, n, rows], dqh_r.at[n, half]))
+        total = dqf[j, rows] + dqr[j, 0, rows].astype(jnp.float32) + dqr[j, 1, rows].astype(jnp.float32)
+        ost[j, 0, half] = total.astype(jnp.bfloat16).reshape(ost.shape[3:])
+        to = oq_ref.at[0, 0, :, :, lanes(me, j)]
+
+        def across(k):
+            xk = lax.rem(x + k, 4)
+            remote(ost.at[j, 0, half, :, xk], to, out_s.at[j, 0], out_r.at[0], (half, h, xk)).start()
+
+        @pl.when(f == half)
+        def _():
+            pltpu.make_async_copy(ost.at[j, 0, half, :, x], to, out_r.at[0]).start()
+
+        pl.when(f != half)(lambda: across(0))
+        for k in range(1, 4):
+            across(k)
 
     def finish_queries(j):
         each(lambda n: await_bytes(dqr.at[j, n], dq_r.at[n, j]))
@@ -232,7 +246,12 @@
             phase_b(2 * n, j, lax.rem(j, 3), qg, kv, es, dps, ms, fin, dka, dva, dqs, dqf)
 
         neighbours_of(one)
-        pl.when(j == nh - 1)(lambda: return_queries(j))
+
+        @pl.when(j == nh - 1)
+        def _():
+            return_half(0)
+            return_half(1)
+
         phase_b(1, j, lax.rem(j, 3), qg, kv, es, dps, ms, fin, dka, dva, dqs, dqf)
         ost[j, 1] = (dka[...] * HD**-0.5).astype(jnp.bfloat16).reshape(ost.shape[2:])
         ost[j, 2] = dva[...].astype(jnp.bfloat16).reshape(ost.shape[2:])
@@ -240,22 +259,17 @@
         leave(j, 2, ov_ref)
 
     def step(t, carry):
-        @pl.when(t + 1 < nh)
-        def _():
-            lend_queries(t + 1)
-
-        pl.when(t == nh - 2)(lambda: return_queries(0))
+        pl.when(t + 1 < nh)(lambda: lend_queries(t + 1))
+
+        pl.when(t == nh - 1)(lambda: return_queries(0))
 
         @pl.when(t < nh)
         def _():
-            @pl.when(t == 0)
-            def _():
-                each(lambda n: lend[n].wait_recv())
-
             for a in range(2):
                 await_bytes(kv.at[t, a], xin_r.at[t, 2 + a])
             phase_a(1, t, lax.rem(t, 3), qg, kv, bias, es, dps, ms, pst)
-            weights_beside(t)
+
+        pl.when(t >= 2)(lambda: gradients(t - 2))
 
         @pl.when(jnp.logical_and(t >= 1, t < nh + 1))
         def _():
@@ -264,18 +278,42 @@
             combine(j, pst, prc, fin)
             each(lambda n: remote(fin.at[j, 1], fin.at[j, 2 - 2 * n], fin_s.at[n, j], fin_r.at[1 - n, j], beside[n]).start())
 
-        pl.when(t >= nh - 1)(lambda: return_queries(t - nh + 2))
-
-        @pl.when(t >= 2)
-        def _():
-            gradients(t - 2)
-
-        pl.when(t == nh)(lambda: finish_queries(0))
+        @pl.when(t < nh)
+        def _():
+            pl.when(t == 0)(lambda: each(lambda n: lend[n].wait_recv()))
+            weights_beside(t)
+
+        @pl.when(t == nh - 1)
+        def _():
+            return_queries(1)
+            finish_queries(0)
+
+        @pl.when(t == nh)
+        def _():
+            return_queries(2)
+            return_queries(3)
+            finish_queries(1)
+
         return carry
 
     lend_queries(0)
+    swap.wait()
+    bias[1] = tab[1]
+    lend = [remote(tab.at[2 * n], bias.at[2 * n], bias_s.at[n], bias_r.at[n], beside[1 - n]) for n in range(2)]
+    each(lambda n: lend[1 - n].start())
+
+    @pl.when(h == 0)
+    def _():
+        blank(0)
+
+    @pl.when(h == NROWS - 1)
+    def _():
+        blank(1)
+
     lax.fori_loop(0, nh + 2, step, 0)
-    lax.fori_loop(1, nh, lambda j, c: (finish_queries(j), c)[1], 0)
+    lax.fori_loop(2, nh - 1, lambda j, c: (finish_queries(j), c)[1], 0)
+    finish_half(0)
+    finish_half(1)
 
     for a, out in enumerate((oq_ref, ok_ref, ov_ref)):
         await_bytes(out, out_r.at[a])
@@ -292,12 +330,14 @@
             await_bytes(qg.at[1, j], halo_s.at[n, j])
             await_bytes(prc.at[j, n], part_s.at[n, j])
             await_bytes(prc.at[j, n], fin_s.at[n, j])
-            await_bytes(dqr.at[j, n], dq_s.at[n, j])
+            pl.when(j < nh - 1)(lambda: await_bytes(dqr.at[j, n], dq_s.at[n, j]))
 
         each(lent)
         return carry
 
     lax.fori_loop(0, nh, settle, 0)
+    for half in range(2):
+        each(lambda n: await_bytes(dqr.at[nh - 1, n, pl.ds(0, 2 * TILE)], dqh_s.at[n, half]))
 
 
 def hand_over(aq, ak, av, bq, bk, bv, room, into, out):
@@ -353,6 +393,7 @@
             dma(()), dma(()),
             dma((2,)), dma((2,)),
             dma(()),
+            dma((2, 2)), dma((2, 2)),
         ],
         compiler_params=pltpu.CompilerParams(
             collective_id=0, has_side_effects=True, vmem_limit_bytes=60 * 1024 * 1024

time: 70.3 us -> 68.7 us (0.977)
  Pallas kernels: 69.5 us -> 67.9 us
    pallas_call x1, Pallas kernels: 67.2 us -> 65.5 us  [local(): pl.pallas_call(functools.partial(kernel, nh), out_shape=(shape, shape, sh...]
where the time goes in v4:
time: 68.7 us; the launch traced here: 68.5 us
  Pallas kernels  67.9 us (99%)
    pallas_call x1, Pallas kernels, local(): pl.pallas_call(functools.partial(kernel, nh), out_shape=(shape, shape, sh...  65.5 us
    pallas_call x1, Pallas kernels, local(): pl.pallas_call(hand_over, out_shape=(shape, shape, shape), in_specs=[any_...  2.34 us

profile of v4, /device:TPU:97, one launch (start us, length us, event | category | flops | bytes accessed | tf_op | source)
XLA Modules:
  0.0 68.5 jit_solution(5800201135258649225)
XLA Ops:
  0.6 65.5 %window_backward.1 = (bf16[1,1,2,32,5120]{4,3,2,1,0:T(8,128)(2,1)}, bf16[1,1,2,32,5120]{4,3,2,1,0:T(8,128)(2,1)}, bf16[1,1,2,32,5120]{4,3,2,1,0:T(8,128)(2,1)}) custom-call(bf16[1,1,2,32,5120]{4,3,2,1,0:T(8,128)(2,1)} %q_ref.1, bf16[1,1,2,32,5120]{4,3,2,1,0:T(8,128)(2,1)} %k_ref.1, bf16[1,1,2,32,5120]{4,3,2,1,0:T(8,128)(2,1)} %v_ref.1, ...), custom_call_target="tpu_custom_call" | custom-call | flops 5033164800 | bytes 4587520 | tf_op jit(solution)/shard_map/window_backward/pallas_call | solution.py:364
  66.2 2.3 %hand_over.1 = (bf16[1,1,2,32,5120]{4,3,2,1,0:T(8,128)(2,1)}, bf16[1,1,2,32,5120]{4,3,2,1,0:T(8,128)(2,1)}, bf16[1,1,2,32,5120]{4,3,2,1,0:T(8,128)(2,1)}) custom-call(bf16[1,1,2,32,5120]{4,3,2,1,0:T(8,128)(2,1)} %get-tuple-element.6.aq, bf16[1,1,2,32,5120]{4,3,2,1,0:T(8,128)(2,1)} %get-tuple-element.7.ak, bf16[1,1,2,32,5120]{4,3,2,1,0:T(8,128)(2,1)} %get-tuple-element.8.av), custom_call_target="tpu_custom_call" | custom-call | tf_op jit(solution)/shard_map/hand_over/pallas_call | solution.py:406

commit v5 on v4

v5 whole, which is shorter than its diff:
```python
import functools

import jax
import jax.numpy as jnp
from jax import lax
from jax.experimental import pallas as pl
from jax.experimental.pallas import tpu as pltpu
from jax.sharding import PartitionSpec as P

MESH = pl.DeviceIdType.MESH
HD = 128
TILE = 128
NROWS = 16
LOG2E = 1.4426950408889634
NONE = -1e30
NT = (((1,), (1,)), ((), ()))
NN = (((1,), (0,)), ((), ()))
TN = (((0,), (0,)), ((), ()))


def dot(a, b, dims):
    return lax.dot_general(a, b, dims, preferred_element_type=jnp.float32)


def phase_a(s, j, p, qg, kv, bias, es, dps, ms, pst):
    scale = LOG2E * HD**-0.5

    def block(f, carry):
        i = 2 * s + f
        q = qg[s, j, 0, f].reshape(2 * TILE, HD)
        g = qg[s, j, 1, f].reshape(2 * TILE, HD)
        peaks, sums, prods = [], [], []
        for kt in range(4):
            k = kv[j, 0, kt // 2, kt % 2].reshape(TILE, HD)
            v = kv[j, 1, kt // 2, kt % 2].reshape(TILE, HD)
            st = dot(k, q, NT) * scale
            m = jnp.max(st, axis=0, keepdims=True)
            e = jnp.exp2(st - m)
            dp = dot(v, g, NT)
            es[p, i, kt] = e
            dps[p, i, kt] = dp
            mb = m + bias[s, f, kt : kt + 1, :]
            ms[p, i, kt : kt + 1, :] = mb
            peaks.append(mb)
            sums.append(jnp.sum(e, axis=0, keepdims=True))
            prods.append(jnp.sum(e * dp, axis=0, keepdims=True))
        top = functools.reduce(jnp.maximum, peaks)
        ws = [jnp.exp2(mb - top) for mb in peaks]
        pst[j, s, 3 * f : 3 * f + 1, :] = top
        pst[j, s, 3 * f + 1 : 3 * f + 2, :] = sum(w * l for w, l in zip(ws, sums))
        pst[j, s, 3 * f + 2 : 3 * f + 3, :] = sum(w * d for w, d in zip(ws, prods))
        return carry

    block(0, 0)
    block(1, 0)


def combine(j, pst, prc, fin):
    for f in range(2):
        rows = slice(3 * f, 3 * f + 3)
        parts = [pst[j, 1, rows], prc[j, 0, rows], prc[j, 1, rows]]
        top = functools.reduce(jnp.maximum, [x[0:1] for x in parts])
        ws = [jnp.exp2(x[0:1] - top) for x in parts]
        total = sum(w * x[1:2] for w, x in zip(ws, parts))
        prod = sum(w * x[2:3] for w, x in zip(ws, parts))
        fin[j, 1, 2 * f : 2 * f + 1, :] = top + jnp.log2(total)
        fin[j, 1, 2 * f + 1 : 2 * f + 2, :] = prod / total


def phase_b(s, j, p, qg, kv, es, dps, ms, fin, dka, dva, dqs, dqf):
    scale = HD**-0.5

    def block(f, carry):
        i = 2 * s + f
        q = qg[s, j, 0, f].reshape(2 * TILE, HD)
        g = qg[s, j, 1, f].reshape(2 * TILE, HD)
        lse = fin[j, s, 2 * f : 2 * f + 1, :]
        delta = fin[j, s, 2 * f + 1 : 2 * f + 2, :]
        probs, grads = [], []
        for kt in range(4):
            r = jnp.exp2(ms[p, i, kt : kt + 1, :] - lse)
            prob = es[p, i, kt] * r
            ds = (prob * (dps[p, i, kt] - delta)).astype(jnp.bfloat16)
            probs.append(prob.astype(jnp.bfloat16))
            grads.append(ds)
        probs, grads = jnp.concatenate(probs), jnp.concatenate(grads)
        dva[...] += dot(probs, g, NN).reshape(dva.shape)
        dka[...] += dot(grads, q, NN).reshape(dka.shape)
        dq = dot(kv[j, 0].reshape(4 * TILE, HD), grads, TN).T * scale
        rows = pl.ds(pl.multiple_of(f * 2 * TILE, 2 * TILE), 2 * TILE)
        if isinstance(s, int):
            dqf[j, rows] = dq
        else:
            dqs[j, s, rows] = dq.astype(jnp.bfloat16)
        return carry

    block(0, 0)
    block(1, 0)


def kernel(nh, q_ref, k_ref, v_ref, g_ref, nb_hbm, oq_ref, ok_ref, ov_ref,
           nb_ref, qg, kv, tab, bias, es, dps, ms, pst, prc, fin, dka, dva, dqs, dqr, dqf, ost,
           xin_s, xin_r, halo_s, halo_r, part_s, part_r, fin_s, fin_r, dq_s, dq_r, out_s, out_r,
           tab_s, tab_r, bias_s, bias_r, nb_s, dqh_s, dqh_r):
    f = lax.axis_index("frames")
    h = lax.axis_index("rows")
    x = lax.axis_index("heads")
    me = x * 2 + f
    beside = (f, jnp.maximum(h - 1, 0), x), (f, jnp.minimum(h + 1, NROWS - 1), x)
    held = h > 0, h < NROWS - 1

    def member(k):
        other = lax.rem(me + k, 8)
        return other, (other % 2, h, other // 2)

    near = pltpu.make_async_copy(nb_hbm, nb_ref, nb_s)
    near.start()
    barrier = pltpu.get_barrier_semaphore()
    for k in range(1, 8):
        pl.semaphore_signal(barrier, inc=1, device_id=member(k)[1], device_id_type=MESH)
    for n in range(2):

        @pl.when(held[n])
        def _():
            pl.semaphore_signal(barrier, inc=1, device_id=beside[n], device_id_type=MESH)

    pl.semaphore_wait(barrier, 7 + held[0].astype(jnp.int32) + held[1].astype(jnp.int32))

    def remote(src, dst, send, recv, device):
        return pltpu.make_async_remote_copy(
            src_ref=src, dst_ref=dst, send_sem=send, recv_sem=recv, device_id=device, device_id_type=MESH
        )

    def await_bytes(ref, sem):
        pltpu.make_async_copy(ref, ref, sem).wait()

    def each(action):
        for n in range(2):
            pl.when(held[n])(functools.partial(action, n))

    def lanes(owner, j):
        return pl.ds(pl.multiple_of((owner * nh + j) * HD, HD), HD)

    def enter(j, pair):
        sides = ((q_ref, qg.at[1, j, 0]), (g_ref, qg.at[1, j, 1])), ((k_ref, kv.at[j, 0]), (v_ref, kv.at[j, 1]))
        for a, (src, dst) in enumerate(sides[pair]):
            to = dst.at[f, :, x]
            recv = xin_r.at[j, 2 * pair + a]
            pltpu.make_async_copy(src.at[0, 0, :, :, lanes(me, j)], to, recv).start()
            for k in range(1, 8):
                other, device = member(k)
                remote(src.at[0, 0, :, :, lanes(other, j)], to, xin_s.at[j, 2 * pair + a], recv, device).start()

    def leave(j, a, out):
        to = out.at[0, 0, :, :, lanes(me, j)]
        pltpu.make_async_copy(ost.at[j, a, f, :, x], to, out_r.at[a]).start()
        for k in range(1, 8):
            other, device = member(k)
            remote(ost.at[j, a, other % 2, :, other // 2], to, out_s.at[j, a], out_r.at[a], device).start()

    def blank(n):
        dqr[:, n] = jnp.zeros_like(dqr[:, n])
        prc[:, n] = jnp.full_like(prc[:, n], NONE)

    def enter_both(j, carry):
        pl.when(j < nh)(lambda: enter(j, 0))
        pl.when(j >= 1)(lambda: enter(j - 1, 1))
        return carry

    enter(0, 0)
    lax.fori_loop(1, nh + 1, enter_both, 0)

    def lend_queries(j):
        for a in range(2):
            await_bytes(qg.at[1, j, a], xin_r.at[j, a])
            each(lambda n: remote(qg.at[1, j, a], qg.at[2 - 2 * n, j, a], halo_s.at[n, j], halo_r.at[1 - n, j], beside[n]).start())

    def return_queries(j):
        each(lambda n: remote(dqs.at[j, 2 * n], dqr.at[j, 1 - n], dq_s.at[n, j], dq_r.at[1 - n, j], beside[n]).start())

    def return_half(half):
        rows = pl.ds(half * 2 * TILE, 2 * TILE)
        each(lambda n: remote(dqs.at[nh - 1, 2 * n, rows], dqr.at[nh - 1, 1 - n, rows], dqh_s.at[n, half], dqh_r.at[1 - n, half], beside[n]).start())

    def finish_half(half):
        j, rows = nh - 1, pl.ds(half * 2 * TILE, 2 * TILE)
        each(lambda n: await_bytes(dqr.at[j, n, rows], dqh_r.at[n, half]))
        total = dqf[j, rows] + dqr[j, 0, rows].astype(jnp.float32) + dqr[j, 1, rows].astype(jnp.float32)
        ost[j, 0, half] = total.astype(jnp.bfloat16).reshape(ost.shape[3:])
        to = oq_ref.at[0, 0, :, :, lanes(me, j)]

        def across(k):
            xk = lax.rem(x + k, 4)
            remote(ost.at[j, 0, half, :, xk], to, out_s.at[j, 0], out_r.at[0], (half, h, xk)).start()

        @pl.when(f == half)
        def _():
            pltpu.make_async_copy(ost.at[j, 0, half, :, x], to, out_r.at[0]).start()

        pl.when(f != half)(lambda: across(0))
        for k in range(1, 4):
            across(k)

    def finish_queries(j):
        each(lambda n: await_bytes(dqr.at[j, n], dq_r.at[n, j]))
        total = dqf[j] + dqr[j, 0].astype(jnp.float32) + dqr[j, 1].astype(jnp.float32)
        ost[j, 0] = total.astype(jnp.bfloat16).reshape(ost.shape[2:])
        leave(j, 0, oq_ref)

    def neighbours_of(action):
        def body(n, carry):
            ahead = jnp.where(n == 0, h - 1, h + 1)
            pl.when(jnp.logical_and(ahead >= 0, ahead < NROWS))(lambda: action(n, (f, ahead, x)))
            return carry

        lax.fori_loop(0, 2, body, 0)

    def weights_beside(j):
        def one(n, device):
            await_bytes(qg.at[2 * n, j], halo_r.at[n, j])
            phase_a(2 * n, j, lax.rem(j, 3), qg, kv, bias, es, dps, ms, pst)
            remote(pst.at[j, 2 * n], prc.at[j, 1 - n], part_s.at[n, j], part_r.at[1 - n, j], device).start()

        neighbours_of(one)

    def gradients(j):
        dka[...] = jnp.zeros_like(dka)
        dva[...] = jnp.zeros_like(dva)

        def one(n, device):
            await_bytes(fin.at[j, 2 * n], fin_r.at[n, j])
            phase_b(2 * n, j, lax.rem(j, 3), qg, kv, es, dps, ms, fin, dka, dva, dqs, dqf)

        neighbours_of(one)

        @pl.when(j == nh - 1)
        def _():
            return_half(0)
            return_half(1)

        phase_b(1, j, lax.rem(j, 3), qg, kv, es, dps, ms, fin, dka, dva, dqs, dqf)
        ost[j, 1] = (dka[...] * HD**-0.5).astype(jnp.bfloat16).reshape(ost.shape[2:])
        ost[j, 2] = dva[...].astype(jnp.bfloat16).reshape(ost.shape[2:])
        leave(j, 1, ok_ref)
        leave(j, 2, ov_ref)

    def step(t, carry):
        pl.when(t + 1 < nh)(lambda: lend_queries(t + 1))

        pl.when(t == nh - 1)(lambda: return_queries(0))

        @pl.when(t < nh)
        def _():
            for a in range(2):
                await_bytes(kv.at[t, a], xin_r.at[t, 2 + a])
            phase_a(1, t, lax.rem(t, 3), qg, kv, bias, es, dps, ms, pst)

        pl.when(t >= 2)(lambda: gradients(t - 2))

        @pl.when(jnp.logical_and(t >= 1, t < nh + 1))
        def _():
            j = t - 1
            each(lambda n: await_bytes(prc.at[j, n], part_r.at[n, j]))
            combine(j, pst, prc, fin)
            each(lambda n: remote(fin.at[j, 1], fin.at[j, 2 - 2 * n], fin_s.at[n, j], fin_r.at[1 - n, j], beside[n]).start())

        @pl.when(t < nh)
        def _():
            pl.when(t == 0)(lambda: each(lambda n: lend[n].wait_recv()))
            weights_beside(t)

        @pl.when(t == nh - 1)
        def _():
            return_queries(1)
            finish_queries(0)

        @pl.when(t == nh)
        def _():
            return_queries(2)
            return_queries(3)
            finish_queries(1)

        return carry

    near.wait()
    for n, dr in enumerate((1, 0, -1)):
        row = h + dr
        inside = jnp.logical_and(row >= 0, row < NROWS)
        for kt in range(4):
            wanted = jnp.where(inside, (kt // 2 * NROWS + row) * 2 + kt % 2, -2)
            for c in range(2):
                found = jnp.where(nb_ref[0, 0, c : c + 1, :] == wanted, 0.0, NONE)
                found = jnp.max(found, axis=-1, keepdims=True)
                tab[n, f, kt : kt + 1, c * TILE : (c + 1) * TILE] = jnp.broadcast_to(found, (1, TILE))
        tab[n, f, 4:8, :] = jnp.zeros((4, 2 * TILE), jnp.float32)
    swap = remote(tab.at[:, f], tab.at[:, f], tab_s, tab_r, (1 - f, h, x))
    swap.start()

    lend_queries(0)
    swap.wait()
    bias[1] = tab[1]
    lend = [remote(tab.at[2 * n], bias.at[2 * n], bias_s.at[n], bias_r.at[n], beside[1 - n]) for n in range(2)]
    each(lambda n: lend[1 - n].start())

    @pl.when(h == 0)
    def _():
        blank(0)

    @pl.when(h == NROWS - 1)
    def _():
        blank(1)

    lax.fori_loop(0, nh + 2, step, 0)
    lax.fori_loop(2, nh - 1, lambda j, c: (finish_queries(j), c)[1], 0)
    finish_half(0)
    finish_half(1)

    each(lambda n: lend[1 - n].wait_send())

    def settle(j, carry):
        sent = dqs.at[j, 0, pl.ds(0, 7 * TILE // 2)]
        for a in range(4):
            await_bytes(sent, xin_s.at[j, a])
        for a in range(3):
            await_bytes(sent, out_s.at[j, a])

        def lent(n):
            await_bytes(qg.at[1, j], halo_s.at[n, j])
            await_bytes(prc.at[j, n], part_s.at[n, j])
            await_bytes(prc.at[j, n], fin_s.at[n, j])
            pl.when(j < nh - 1)(lambda: await_bytes(dqr.at[j, n], dq_s.at[n, j]))

        each(lent)
        return carry

    lax.fori_loop(0, nh, settle, 0)
    for half in range(2):
        each(lambda n: await_bytes(dqr.at[nh - 1, n, pl.ds(0, 2 * TILE)], dqh_s.at[n, half]))
    for a, out in enumerate((oq_ref, ok_ref, ov_ref)):
        await_bytes(out, out_r.at[a])


def hand_over(aq, ak, av, bq, bk, bv, out):
    copies = [pltpu.make_async_copy(a, b, out.at[n]) for n, (a, b) in enumerate(((aq, bq), (ak, bk), (av, bv)))]
    for copy in copies:
        copy.start()
    for copy in copies:
        copy.wait()


def local(queries, keys, values, out_grad, neighbours):
    nh = queries.shape[-1] // HD // 8
    tiles = (2, 2, 4, TILE // 4, HD)
    bf, f32 = jnp.bfloat16, jnp.float32
    dma = pltpu.SemaphoreType.DMA
    any_spec = pl.BlockSpec(memory_space=pl.ANY)
    shape = jax.ShapeDtypeStruct(queries.shape, bf)
    products = 5 * 512 * 1536 * HD * nh
    grads = pl.pallas_call(
        functools.partial(kernel, nh),
        out_shape=(pltpu.VMEM(queries.shape, bf),) * 3,
        in_specs=[any_spec] * 5,
        out_specs=[pl.BlockSpec(memory_space=pltpu.VMEM)] * 3,
        scratch_shapes=[
            pltpu.VMEM(neighbours.shape, jnp.int32),
            pltpu.VMEM((3, nh, 2) + tiles, bf),
            pltpu.VMEM((nh, 2) + tiles, bf),
            pltpu.VMEM((3, 2, 8, 256), f32),
            pltpu.VMEM((3, 2, 8, 256), f32),
            pltpu.VMEM((3, 6, 4, TILE, 256), f32),
            pltpu.VMEM((3, 6, 4, TILE, 256), f32),
            pltpu.VMEM((3, 6, 8, 256), f32),
            pltpu.VMEM((nh, 3, 8, 256), f32),
            pltpu.VMEM((nh, 2, 8, 256), f32),
            pltpu.VMEM((nh, 3, 8, 256), f32),
            pltpu.VMEM((4, TILE, HD), f32),
            pltpu.VMEM((4, TILE, HD), f32),
            pltpu.VMEM((nh, 3, 512, HD), bf),
            pltpu.VMEM((nh, 2, 512, HD), bf),
            pltpu.VMEM((nh, 512, HD), f32),
            pltpu.VMEM((nh, 3) + tiles, bf),
            dma((nh, 4)), dma((nh, 4)),
            dma((2, nh)), dma((2, nh)),
            dma((2, nh)), dma((2, nh)),
            dma((2, nh)), dma((2, nh)),
            dma((2, nh)), dma((2, nh)),
            dma((nh, 3)), dma((3,)),
            dma(()), dma(()),
            dma((2,)), dma((2,)),
            dma(()),
            dma((2, 2)), dma((2, 2)),
        ],
        compiler_params=pltpu.CompilerParams(
            collective_id=0, has_side_effects=True, vmem_limit_bytes=48 * 1024 * 1024
        ),
        cost_estimate=pl.CostEstimate(
            flops=2 * products, bytes_accessed=7 * 2 * queries.size, transcendentals=512 * 1536 * nh
        ),
        name="window_backward",
    )(*(pltpu.with_memory_space_constraint(a, pltpu.HBM) for a in (queries, keys, values, out_grad, neighbours)))
    return pl.pallas_call(
        hand_over,
        out_shape=(shape, shape, shape),
        in_specs=[pl.BlockSpec(memory_space=pltpu.VMEM)] * 3,
        out_specs=[any_spec] * 3,
        scratch_shapes=[dma((3,))],
        name="hand_over",
    )(*(pltpu.with_memory_space_constraint(a, pltpu.VMEM) for a in grads))


def solution(mesh):
    whole = P("frames", "rows", None, "heads", None)
    return jax.shard_map(
        local,
        mesh=mesh,
        in_specs=(whole, whole, whole, whole, P("frames", "rows", None, None)),
        out_specs=(whole, whole, whole),
        check_vma=False,
    )
```

time: 68.7 us -> 65.9 us (0.959)
  Pallas kernels: 67.9 us -> 65.2 us
    pallas_call x2, Pallas kernels: 67.9 us -> 65.2 us  [the longest x1 63.9 us: local(): pl.pallas_call(functools.partial(kernel, nh), out_shape=(pltpu.VMEM(queri...]
where the time goes in v5:
time: 65.9 us; the launch traced here: 65.8 us
  Pallas kernels  65.2 us (99%)
    pallas_call x1, Pallas kernels, local(): pl.pallas_call(functools.partial(kernel, nh), out_shape=(pltpu.VMEM(queri...  63.9 us

profile of v5, /device:TPU:97, one launch (start us, length us, event | category | flops | bytes accessed | tf_op | source)
XLA Modules:
  0.0 65.8 jit_solution(17768582926962222820)
XLA Ops:
  0.6 63.9 %window_backward.1 = (bf16[1,1,2,32,5120]{4,3,2,1,0:T(8,128)(2,1)S(1)}, bf16[1,1,2,32,5120]{4,3,2,1,0:T(8,128)(2,1)S(1)}, bf16[1,1,2,32,5120]{4,3,2,1,0:T(8,128)(2,1)S(1)}) custom-call(bf16[1,1,2,32,5120]{4,3,2,1,0:T(8,128)(2,1)} %q_ref.1, bf16[1,1,2,32,5120]{4,3,2,1,0:T(8,128)(2,1)} %k_ref.1, bf16[1,1,2,32,5120]{4,3,2,1,0:T(8,128)(2,1)} %v_ref.1, ...), custom_call_target="tpu_custom_call" | custom-call | flops 5033164800 | bytes 4587520 | tf_op jit(solution)/shard_map/window_backward/pallas_call | solution.py:359
  64.5 1.3 %hand_over.1 = (bf16[1,1,2,32,5120]{4,3,2,1,0:T(8,128)(2,1)}, bf16[1,1,2,32,5120]{4,3,2,1,0:T(8,128)(2,1)}, bf16[1,1,2,32,5120]{4,3,2,1,0:T(8,128)(2,1)}) custom-call(bf16[1,1,2,32,5120]{4,3,2,1,0:T(8,128)(2,1)S(1)} %get-tuple-element.6.aq, bf16[1,1,2,32,5120]{4,3,2,1,0:T(8,128)(2,1)S(1)} %get-tuple-element.7.ak, ...), custom_call_target="tpu_custom_call" | custom-call | tf_op jit(solution)/shard_map/hand_over/pallas_call | solution.py:401

commit v6 on v5

--- a/solution.py
+++ b/solution.py
@@ -39,16 +39,16 @@
             dp = dot(v, g, NT)
             es[p, i, kt] = e
             dps[p, i, kt] = dp
-            mb = m + bias[s, f, kt : kt + 1, :]
+            mb = m + bias[s, 4 * f + kt : 4 * f + kt + 1, :]
             ms[p, i, kt : kt + 1, :] = mb
             peaks.append(mb)
             sums.append(jnp.sum(e, axis=0, keepdims=True))
             prods.append(jnp.sum(e * dp, axis=0, keepdims=True))
         top = functools.reduce(jnp.maximum, peaks)
         ws = [jnp.exp2(mb - top) for mb in peaks]
-        pst[j, s, 3 * f : 3 * f + 1, :] = top
-        pst[j, s, 3 * f + 1 : 3 * f + 2, :] = sum(w * l for w, l in zip(ws, sums))
-        pst[j, s, 3 * f + 2 : 3 * f + 3, :] = sum(w * d for w, d in zip(ws, prods))
+        total = sum(w * l for w, l in zip(ws, sums))
+        pst[j, s, 2 * f : 2 * f + 1, :] = top + jnp.log2(total)
+        pst[j, s, 2 * f + 1 : 2 * f + 2, :] = sum(w * d for w, d in zip(ws, prods)) / total
         return carry
 
     block(0, 0)
@@ -57,12 +57,12 @@
 
 def combine(j, pst, prc, fin):
     for f in range(2):
-        rows = slice(3 * f, 3 * f + 3)
+        rows = slice(2 * f, 2 * f + 2)
         parts = [pst[j, 1, rows], prc[j, 0, rows], prc[j, 1, rows]]
         top = functools.reduce(jnp.maximum, [x[0:1] for x in parts])
         ws = [jnp.exp2(x[0:1] - top) for x in parts]
-        total = sum(w * x[1:2] for w, x in zip(ws, parts))
-        prod = sum(w * x[2:3] for w, x in zip(ws, parts))
+        total = sum(ws)
+        prod = sum(w * x[1:2] for w, x in zip(ws, parts))
         fin[j, 1, 2 * f : 2 * f + 1, :] = top + jnp.log2(total)
         fin[j, 1, 2 * f + 1 : 2 * f + 2, :] = prod / total
 
@@ -99,9 +99,9 @@
 
 
 def kernel(nh, q_ref, k_ref, v_ref, g_ref, nb_hbm, oq_ref, ok_ref, ov_ref,
-           nb_ref, qg, kv, tab, bias, es, dps, ms, pst, prc, fin, dka, dva, dqs, dqr, dqf, ost,
+           nb_ref, qg, kv, tab, lent, bias, es, dps, ms, pst, prc, fin, dka, dva, dqs, dqr, dqf, ost,
            xin_s, xin_r, halo_s, halo_r, part_s, part_r, fin_s, fin_r, dq_s, dq_r, out_s, out_r,
-           tab_s, tab_r, bias_s, bias_r, nb_s, dqh_s, dqh_r):
+           tab_s, tab_r, bias_s, bias_r, nb_s, dqh_s, dqh_r, early_r):
     f = lax.axis_index("frames")
     h = lax.axis_index("rows")
     x = lax.axis_index("heads")
@@ -141,9 +141,9 @@
     def lanes(owner, j):
         return pl.ds(pl.multiple_of((owner * nh + j) * HD, HD), HD)
 
-    def enter(j, pair):
+    def enter(j, pair, skip=0):
         sides = ((q_ref, qg.at[1, j, 0]), (g_ref, qg.at[1, j, 1])), ((k_ref, kv.at[j, 0]), (v_ref, kv.at[j, 1]))
-        for a, (src, dst) in enumerate(sides[pair]):
+        for a, (src, dst) in list(enumerate(sides[pair]))[skip:]:
             to = dst.at[f, :, x]
             recv = xin_r.at[j, 2 * pair + a]
             pltpu.make_async_copy(src.at[0, 0, :, :, lanes(me, j)], to, recv).start()
@@ -151,6 +151,15 @@
                 other, device = member(k)
                 remote(src.at[0, 0, :, :, lanes(other, j)], to, xin_s.at[j, 2 * pair + a], recv, device).start()
 
+    def enter_first():
+        for c in range(2):
+            to = qg.at[1, 0, 0, f, c, x]
+            recv = xin_r.at[0, 0] if c else early_r
+            pltpu.make_async_copy(q_ref.at[0, 0, c, :, lanes(me, 0)], to, recv).start()
+            for k in range(1, 8):
+                other, device = member(k)
+                remote(q_ref.at[0, 0, c, :, lanes(other, 0)], to, xin_s.at[0, 0], recv, device).start()
+
     def leave(j, a, out):
         to = out.at[0, 0, :, :, lanes(me, j)]
         pltpu.make_async_copy(ost.at[j, a, f, :, x], to, out_r.at[a]).start()
@@ -167,11 +176,17 @@
         pl.when(j >= 1)(lambda: enter(j - 1, 1))
         return carry
 
-    enter(0, 0)
+    enter_first()
+    enter(0, 0, 1)
     lax.fori_loop(1, nh + 1, enter_both, 0)
 
-    def lend_queries(j):
-        for a in range(2):
+    def lend_first():
+        for c in range(2):
+            await_bytes(qg.at[1, 0, 0, :, c], xin_r.at[0, 0] if c else early_r)
+            each(lambda n: remote(qg.at[1, 0, 0, :, c], qg.at[2 - 2 * n, 0, 0, :, c], halo_s.at[n, 0], halo_r.at[1 - n, 0], beside[n]).start())
+
+    def lend_queries(j, skip=0):
+        for a in range(skip, 2):
             await_bytes(qg.at[1, j, a], xin_r.at[j, a])
             each(lambda n: remote(qg.at[1, j, a], qg.at[2 - 2 * n, j, a], halo_s.at[n, j], halo_r.at[1 - n, j], beside[n]).start())
 
@@ -255,7 +270,10 @@
                 await_bytes(kv.at[t, a], xin_r.at[t, 2 + a])
             phase_a(1, t, lax.rem(t, 3), qg, kv, bias, es, dps, ms, pst)
 
-        pl.when(t >= 2)(lambda: gradients(t - 2))
+        @pl.when(t < nh)
+        def _():
+            pl.when(t == 0)(lambda: each(lambda n: lend[n].wait_recv()))
+            weights_beside(t)
 
         @pl.when(jnp.logical_and(t >= 1, t < nh + 1))
         def _():
@@ -264,21 +282,12 @@
             combine(j, pst, prc, fin)
             each(lambda n: remote(fin.at[j, 1], fin.at[j, 2 - 2 * n], fin_s.at[n, j], fin_r.at[1 - n, j], beside[n]).start())
 
-        @pl.when(t < nh)
-        def _():
-            pl.when(t == 0)(lambda: each(lambda n: lend[n].wait_recv()))
-            weights_beside(t)
-
-        @pl.when(t == nh - 1)
-        def _():
-            return_queries(1)
-            finish_queries(0)
-
-        @pl.when(t == nh)
-        def _():
-            return_queries(2)
-            return_queries(3)
-            finish_queries(1)
+        pl.when(t == nh - 1)(lambda: return_queries(1))
+        pl.when(t == nh)(lambda: return_queries(2))
+        pl.when(t == nh)(lambda: finish_queries(0))
+        pl.when(t >= 2)(lambda: gradients(t - 2))
+        pl.when(t == nh)(lambda: return_queries(3))
+        pl.when(t == nh)(lambda: finish_queries(1))
 
         return carry
 
@@ -292,14 +301,16 @@
                 found = jnp.where(nb_ref[0, 0, c : c + 1, :] == wanted, 0.0, NONE)
                 found = jnp.max(found, axis=-1, keepdims=True)
                 tab[n, f, kt : kt + 1, c * TILE : (c + 1) * TILE] = jnp.broadcast_to(found, (1, TILE))
-        tab[n, f, 4:8, :] = jnp.zeros((4, 2 * TILE), jnp.float32)
     swap = remote(tab.at[:, f], tab.at[:, f], tab_s, tab_r, (1 - f, h, x))
     swap.start()
 
-    lend_queries(0)
+    lend_first()
+    lend_queries(0, 1)
     swap.wait()
-    bias[1] = tab[1]
-    lend = [remote(tab.at[2 * n], bias.at[2 * n], bias_s.at[n], bias_r.at[n], beside[1 - n]) for n in range(2)]
+    for g in range(2):
+        lent[:, 4 * g : 4 * g + 4, :] = tab[:, g]
+    bias[1] = lent[1]
+    lend = [remote(lent.at[2 * n], bias.at[2 * n], bias_s.at[n], bias_r.at[n], beside[1 - n]) for n in range(2)]
     each(lambda n: lend[1 - n].start())
 
     @pl.when(h == 0)
@@ -324,13 +335,13 @@
         for a in range(3):
             await_bytes(sent, out_s.at[j, a])
 
-        def lent(n):
+        def settle_beside(n):
             await_bytes(qg.at[1, j], halo_s.at[n, j])
             await_bytes(prc.at[j, n], part_s.at[n, j])
             await_bytes(prc.at[j, n], fin_s.at[n, j])
             pl.when(j < nh - 1)(lambda: await_bytes(dqr.at[j, n], dq_s.at[n, j]))
 
-        each(lent)
+        each(settle_beside)
         return carry
 
     lax.fori_loop(0, nh, settle, 0)
@@ -365,14 +376,15 @@
             pltpu.VMEM(neighbours.shape, jnp.int32),
             pltpu.VMEM((3, nh, 2) + tiles, bf),
             pltpu.VMEM((nh, 2) + tiles, bf),
-            pltpu.VMEM((3, 2, 8, 256), f32),
-            pltpu.VMEM((3, 2, 8, 256), f32),
+            pltpu.VMEM((3, 2, 4, 256), f32),
+            pltpu.VMEM((3, 8, 256), f32),
+            pltpu.VMEM((3, 8, 256), f32),
             pltpu.VMEM((3, 6, 4, TILE, 256), f32),
             pltpu.VMEM((3, 6, 4, TILE, 256), f32),
             pltpu.VMEM((3, 6, 8, 256), f32),
-            pltpu.VMEM((nh, 3, 8, 256), f32),
-            pltpu.VMEM((nh, 2, 8, 256), f32),
-            pltpu.VMEM((nh, 3, 8, 256), f32),
+            pltpu.VMEM((nh, 3, 4, 256), f32),
+            pltpu.VMEM((nh, 2, 4, 256), f32),
+            pltpu.VMEM((nh, 3, 4, 256), f32),
             pltpu.VMEM((4, TILE, HD), f32),
             pltpu.VMEM((4, TILE, HD), f32),
             pltpu.VMEM((nh, 3, 512, HD), bf),
@@ -389,6 +401,7 @@
             dma((2,)), dma((2,)),
             dma(()),
             dma((2, 2)), dma((2, 2)),
+            dma(()),
         ],
         compiler_params=pltpu.CompilerParams(
             collective_id=0, has_side_effects=True, vmem_limit_bytes=48 * 1024 * 1024

time: 65.9 us -> 64.1 us (0.973)
  Pallas kernels: 65.2 us -> 63.4 us
    pallas_call x1, Pallas kernels: 63.9 us -> 62.1 us  [local(): pl.pallas_call(functools.partial(kernel, nh), out_shape=(pltpu.VMEM(queri...]
where the time goes in v6:
time: 64.1 us; the launch traced here: 64 us
  Pallas kernels  63.4 us (99%)
    pallas_call x1, Pallas kernels, local(): pl.pallas_call(functools.partial(kernel, nh), out_shape=(pltpu.VMEM(queri...  62.1 us
    pallas_call x1, Pallas kernels, local(): pl.pallas_call(hand_over, out_shape=(shape, shape, shape), in_specs=[pl.B...  1.3 us

profile of v6, /device:TPU:97, one launch (start us, length us, event | category | flops | bytes accessed | tf_op | source)
XLA Modules:
  0.0 64.0 jit_solution(7758229325550011422)
XLA Ops:
  0.6 62.1 %window_backward.1 = (bf16[1,1,2,32,5120]{4,3,2,1,0:T(8,128)(2,1)S(1)}, bf16[1,1,2,32,5120]{4,3,2,1,0:T(8,128)(2,1)S(1)}, bf16[1,1,2,32,5120]{4,3,2,1,0:T(8,128)(2,1)S(1)}) custom-call(bf16[1,1,2,32,5120]{4,3,2,1,0:T(8,128)(2,1)} %q_ref.1, bf16[1,1,2,32,5120]{4,3,2,1,0:T(8,128)(2,1)} %k_ref.1, bf16[1,1,2,32,5120]{4,3,2,1,0:T(8,128)(2,1)} %v_ref.1, ...), custom_call_target="tpu_custom_call" | custom-call | flops 5033164800 | bytes 4587520 | tf_op jit(solution)/shard_map/window_backward/pallas_call | solution.py:370
  62.7 1.3 %hand_over.1 = (bf16[1,1,2,32,5120]{4,3,2,1,0:T(8,128)(2,1)}, bf16[1,1,2,32,5120]{4,3,2,1,0:T(8,128)(2,1)}, bf16[1,1,2,32,5120]{4,3,2,1,0:T(8,128)(2,1)}) custom-call(bf16[1,1,2,32,5120]{4,3,2,1,0:T(8,128)(2,1)S(1)} %get-tuple-element.6.aq, bf16[1,1,2,32,5120]{4,3,2,1,0:T(8,128)(2,1)S(1)} %get-tuple-element.7.ak, ...), custom_call_target="tpu_custom_call" | custom-call | tf_op jit(solution)/shard_map/hand_over/pallas_call | solution.py:414

commit v7 on v6

--- a/solution.py
+++ b/solution.py
@@ -185,8 +185,8 @@
             await_bytes(qg.at[1, 0, 0, :, c], xin_r.at[0, 0] if c else early_r)
             each(lambda n: remote(qg.at[1, 0, 0, :, c], qg.at[2 - 2 * n, 0, 0, :, c], halo_s.at[n, 0], halo_r.at[1 - n, 0], beside[n]).start())
 
-    def lend_queries(j, skip=0):
-        for a in range(skip, 2):
+    def lend_queries(j, start, stop):
+        for a in range(start, stop):
             await_bytes(qg.at[1, j, a], xin_r.at[j, a])
             each(lambda n: remote(qg.at[1, j, a], qg.at[2 - 2 * n, j, a], halo_s.at[n, j], halo_r.at[1 - n, j], beside[n]).start())
 
@@ -260,20 +260,13 @@
         leave(j, 2, ov_ref)
 
     def step(t, carry):
-        pl.when(t + 1 < nh)(lambda: lend_queries(t + 1))
-
-        pl.when(t == nh - 1)(lambda: return_queries(0))
-
-        @pl.when(t < nh)
-        def _():
-            for a in range(2):
-                await_bytes(kv.at[t, a], xin_r.at[t, 2 + a])
-            phase_a(1, t, lax.rem(t, 3), qg, kv, bias, es, dps, ms, pst)
-
-        @pl.when(t < nh)
-        def _():
-            pl.when(t == 0)(lambda: each(lambda n: lend[n].wait_recv()))
-            weights_beside(t)
+        pl.when(t + 1 < nh)(lambda: lend_queries(t + 1, 0, 1))
+
+        @pl.when(t >= nh - 2)
+        def _():
+            low = jnp.where(t < nh, t - nh + 2, t - 2)
+            high = jnp.where(t == nh - 2, 1, t - 1)
+            lax.fori_loop(low, high, lambda j, c: (gradients(j), c)[1], 0)
 
         @pl.when(jnp.logical_and(t >= 1, t < nh + 1))
         def _():
@@ -283,11 +276,23 @@
             each(lambda n: remote(fin.at[j, 1], fin.at[j, 2 - 2 * n], fin_s.at[n, j], fin_r.at[1 - n, j], beside[n]).start())
 
         pl.when(t == nh - 1)(lambda: return_queries(1))
-        pl.when(t == nh)(lambda: return_queries(2))
-        pl.when(t == nh)(lambda: finish_queries(0))
-        pl.when(t >= 2)(lambda: gradients(t - 2))
+        pl.when(t + 1 < nh)(lambda: lend_queries(t + 1, 1, 2))
+
+        @pl.when(t < nh)
+        def _():
+            for a in range(2):
+                await_bytes(kv.at[t, a], xin_r.at[t, 2 + a])
+            phase_a(1, t, lax.rem(t, 3), qg, kv, bias, es, dps, ms, pst)
+            pl.when(t == 0)(lambda: each(lambda n: lend[n].wait_recv()))
+            weights_beside(t)
+
+        pl.when(t == nh - 2)(lambda: return_queries(0))
+        pl.when(t == nh - 1)(lambda: return_queries(2))
         pl.when(t == nh)(lambda: return_queries(3))
-        pl.when(t == nh)(lambda: finish_queries(1))
+
+        @pl.when(jnp.logical_or(t == nh - 1, t == nh))
+        def _():
+            lax.fori_loop(t - nh + 1, 2 * (t - nh) + 3, lambda j, c: (finish_queries(j), c)[1], 0)
 
         return carry
 
@@ -305,7 +310,7 @@
     swap.start()
 
     lend_first()
-    lend_queries(0, 1)
+    lend_queries(0, 1, 2)
     swap.wait()
     for g in range(2):
         lent[:, 4 * g : 4 * g + 4, :] = tab[:, g]
@@ -322,7 +327,7 @@
         blank(1)
 
     lax.fori_loop(0, nh + 2, step, 0)
-    lax.fori_loop(2, nh - 1, lambda j, c: (finish_queries(j), c)[1], 0)
+    finish_queries(3)
     finish_half(0)
     finish_half(1)
 

time: 64.1 us -> 63.8 us (level)
  no operation moved by 1% of the time
where the time goes in v7:
time: 63.8 us; the launch traced here: 63.7 us
  Pallas kernels  63 us (99%)
  between operations  0.64 us (1%)
    pallas_call x1, Pallas kernels, local(): pl.pallas_call(functools.partial(kernel, nh), out_shape=(pltpu.VMEM(queri...  61.7 us
    pallas_call x1, Pallas kernels, local(): pl.pallas_call(hand_over, out_shape=(shape, shape, shape), in_specs=[pl.B...  1.3 us

profile of v7, /device:TPU:97, one launch (start us, length us, event | category | flops | bytes accessed | tf_op | source)
XLA Modules:
  0.0 63.7 jit_solution(7493598982703820920)
XLA Ops:
  0.6 61.7 %window_backward.1 = (bf16[1,1,2,32,5120]{4,3,2,1,0:T(8,128)(2,1)S(1)}, bf16[1,1,2,32,5120]{4,3,2,1,0:T(8,128)(2,1)S(1)}, bf16[1,1,2,32,5120]{4,3,2,1,0:T(8,128)(2,1)S(1)}) custom-call(bf16[1,1,2,32,5120]{4,3,2,1,0:T(8,128)(2,1)} %q_ref.1, bf16[1,1,2,32,5120]{4,3,2,1,0:T(8,128)(2,1)} %k_ref.1, bf16[1,1,2,32,5120]{4,3,2,1,0:T(8,128)(2,1)} %v_ref.1, ...), custom_call_target="tpu_custom_call" | custom-call | flops 5033164800 | bytes 4587520 | tf_op jit(solution)/shard_map/window_backward/pallas_call | solution.py:375
  62.4 1.3 %hand_over.1 = (bf16[1,1,2,32,5120]{4,3,2,1,0:T(8,128)(2,1)}, bf16[1,1,2,32,5120]{4,3,2,1,0:T(8,128)(2,1)}, bf16[1,1,2,32,5120]{4,3,2,1,0:T(8,128)(2,1)}) custom-call(bf16[1,1,2,32,5120]{4,3,2,1,0:T(8,128)(2,1)S(1)} %get-tuple-element.6.aq, bf16[1,1,2,32,5120]{4,3,2,1,0:T(8,128)(2,1)S(1)} %get-tuple-element.7.ak, ...), custom_call_target="tpu_custom_call" | custom-call | tf_op jit(solution)/shard_map/hand_over/pallas_call | solution.py:419

commit v8 on v7

--- a/solution.py
+++ b/solution.py
@@ -110,11 +110,10 @@
     held = h > 0, h < NROWS - 1
 
     def member(k):
-        other = lax.rem(me + k, 8)
-        return other, (other % 2, h, other // 2)
-
-    near = pltpu.make_async_copy(nb_hbm, nb_ref, nb_s)
-    near.start()
+        across, other_core = ((1, 0), (3, 0), (2, 0), (1, 1), (3, 1), (2, 1), (0, 1))[k - 1]
+        peer, core = lax.rem(x + across, 4), lax.rem(f + other_core, 2)
+        return peer * 2 + core, (core, h, peer)
+
     barrier = pltpu.get_barrier_semaphore()
     for k in range(1, 8):
         pl.semaphore_signal(barrier, inc=1, device_id=member(k)[1], device_id_type=MESH)
@@ -124,6 +123,8 @@
         def _():
             pl.semaphore_signal(barrier, inc=1, device_id=beside[n], device_id_type=MESH)
 
+    near = pltpu.make_async_copy(nb_hbm, nb_ref, nb_s)
+    near.start()
     pl.semaphore_wait(barrier, 7 + held[0].astype(jnp.int32) + held[1].astype(jnp.int32))
 
     def remote(src, dst, send, recv, device):

time: 63.8 us -> 63.5 us (level)
  no operation moved by 1% of the time
where the time goes in v8:
time: 63.5 us; the launch traced here: 63.4 us
  Pallas kernels  62.8 us (99%)
  between operations  0.64 us (1%)
    pallas_call x1, Pallas kernels, local(): pl.pallas_call(functools.partial(kernel, nh), out_shape=(pltpu.VMEM(queri...  61.5 us
    pallas_call x1, Pallas kernels, local(): pl.pallas_call(hand_over, out_shape=(shape, shape, shape), in_specs=[pl.B...  1.3 us

profile of v8, /device:TPU:97, one launch (start us, length us, event | category | flops | bytes accessed | tf_op | source)
XLA Modules:
  0.0 63.4 jit_solution(12298655270236634396)
XLA Ops:
  0.6 61.5 %window_backward.1 = (bf16[1,1,2,32,5120]{4,3,2,1,0:T(8,128)(2,1)S(1)}, bf16[1,1,2,32,5120]{4,3,2,1,0:T(8,128)(2,1)S(1)}, bf16[1,1,2,32,5120]{4,3,2,1,0:T(8,128)(2,1)S(1)}) custom-call(bf16[1,1,2,32,5120]{4,3,2,1,0:T(8,128)(2,1)} %q_ref.1, bf16[1,1,2,32,5120]{4,3,2,1,0:T(8,128)(2,1)} %k_ref.1, bf16[1,1,2,32,5120]{4,3,2,1,0:T(8,128)(2,1)} %v_ref.1, ...), custom_call_target="tpu_custom_call" | custom-call | flops 5033164800 | bytes 4587520 | tf_op jit(solution)/shard_map/window_backward/pallas_call | solution.py:376
  62.1 1.3 %hand_over.1 = (bf16[1,1,2,32,5120]{4,3,2,1,0:T(8,128)(2,1)}, bf16[1,1,2,32,5120]{4,3,2,1,0:T(8,128)(2,1)}, bf16[1,1,2,32,5120]{4,3,2,1,0:T(8,128)(2,1)}) custom-call(bf16[1,1,2,32,5120]{4,3,2,1,0:T(8,128)(2,1)S(1)} %get-tuple-element.6.aq, bf16[1,1,2,32,5120]{4,3,2,1,0:T(8,128)(2,1)S(1)} %get-tuple-element.7.ak, ...), custom_call_target="tpu_custom_call" | custom-call | tf_op jit(solution)/shard_map/hand_over/pallas_call | solution.py:420

commit v9 on v8

--- a/solution.py
+++ b/solution.py
@@ -269,6 +269,12 @@
             high = jnp.where(t == nh - 2, 1, t - 1)
             lax.fori_loop(low, high, lambda j, c: (gradients(j), c)[1], 0)
 
+        @pl.when(t < nh)
+        def _():
+            for a in range(2):
+                await_bytes(kv.at[t, a], xin_r.at[t, 2 + a])
+            phase_a(1, t, lax.rem(t, 3), qg, kv, bias, es, dps, ms, pst)
+
         @pl.when(jnp.logical_and(t >= 1, t < nh + 1))
         def _():
             j = t - 1
@@ -281,9 +287,6 @@
 
         @pl.when(t < nh)
         def _():
-            for a in range(2):
-                await_bytes(kv.at[t, a], xin_r.at[t, 2 + a])
-            phase_a(1, t, lax.rem(t, 3), qg, kv, bias, es, dps, ms, pst)
             pl.when(t == 0)(lambda: each(lambda n: lend[n].wait_recv()))
             weights_beside(t)
 

time: 63.5 us -> 63.9 us (level)
  no operation moved by 1% of the time
where the time goes in v9:
time: 63.9 us; the launch traced here: 63.7 us
  Pallas kernels  63.1 us (99%)
  between operations  0.64 us (1%)
    pallas_call x1, Pallas kernels, local(): pl.pallas_call(functools.partial(kernel, nh), out_shape=(pltpu.VMEM(queri...  61.8 us
    pallas_call x1, Pallas kernels, local(): pl.pallas_call(hand_over, out_shape=(shape, shape, shape), in_specs=[pl.B...  1.3 us

profile of v9, /device:TPU:97, one launch (start us, length us, event | category | flops | bytes accessed | tf_op | source)
XLA Modules:
  0.0 63.7 jit_solution(777229754618382697)
XLA Ops:
  0.6 61.8 %window_backward.1 = (bf16[1,1,2,32,5120]{4,3,2,1,0:T(8,128)(2,1)S(1)}, bf16[1,1,2,32,5120]{4,3,2,1,0:T(8,128)(2,1)S(1)}, bf16[1,1,2,32,5120]{4,3,2,1,0:T(8,128)(2,1)S(1)}) custom-call(bf16[1,1,2,32,5120]{4,3,2,1,0:T(8,128)(2,1)} %q_ref.1, bf16[1,1,2,32,5120]{4,3,2,1,0:T(8,128)(2,1)} %k_ref.1, bf16[1,1,2,32,5120]{4,3,2,1,0:T(8,128)(2,1)} %v_ref.1, ...), custom_call_target="tpu_custom_call" | custom-call | flops 5033164800 | bytes 4587520 | tf_op jit(solution)/shard_map/window_backward/pallas_call | solution.py:379
  62.5 1.3 %hand_over.1 = (bf16[1,1,2,32,5120]{4,3,2,1,0:T(8,128)(2,1)}, bf16[1,1,2,32,5120]{4,3,2,1,0:T(8,128)(2,1)}, bf16[1,1,2,32,5120]{4,3,2,1,0:T(8,128)(2,1)}) custom-call(bf16[1,1,2,32,5120]{4,3,2,1,0:T(8,128)(2,1)S(1)} %get-tuple-element.6.aq, bf16[1,1,2,32,5120]{4,3,2,1,0:T(8,128)(2,1)S(1)} %get-tuple-element.7.ak, ...), custom_call_target="tpu_custom_call" | custom-call | tf_op jit(solution)/shard_map/hand_over/pallas_call | solution.py:423
